TPU v7x, 32 devices: a whole 2x2x4 slice. The times are simulated.
32 devices in a mesh: ga: 4 (over y, core), band: 8 (over z, x).
Axes of the slice: x: 2, y: 2, z: 4, core: 2. Of those that a mesh axis runs over, the one named last changes fastest.
Arguments:
- coeffs: float32 [8, 4096, 128], P('band', 'ga'), may hold values from -6 to 6
- potential: bfloat16 [256, 256, 256], P('ga'), may hold values from -2 to 1
- stick_cells: int32 [4096], replicated, may hold values from 0 to 65535, as said below
- block: bfloat16 [64, 524288], P('band', 'ga'), may hold values from -6 to 6
- rotation: bfloat16 [64, 8], P('band'), may hold values from -2 to 2
Outputs:
- h_coeffs: float32 [8, 4096, 128], P('band', 'ga')
- rotated: bfloat16 [64, 524288], P('band', 'ga')
Inputs may be any that keep to these rules, and one draw needn't show every extreme that they name: `stick_cells`: distinct cells: the 4096 cells of the 256 x 256 plane nearest to zero frequency in wrapped distance, ties at the rim broken at random, listed in random order.
All inputs are finite; a program needn't handle non-finite values.
Results may differ from a plain program's by a relative error of at most 0.0039.
Values may be sent and summed in bfloat16 or wider, within the bound.
A program may use at most 128 MiB of HBM per device.

v0:
```python
import functools
import math

import jax
import jax.numpy as jnp
import numpy as np
from jax import lax
from jax.experimental import pallas as pl
from jax.experimental.pallas import tpu as pltpu
from jax.sharding import PartitionSpec as P

BF16 = jnp.bfloat16
F32 = jnp.float32
LEVEL = -0.5


def hartley(count):
    index_row = np.arange(count, dtype=np.int64)
    angles = (index_row[:, None] * index_row[None, :] % count) * (2.0 * math.pi / count)
    return (np.cos(angles) + np.sin(angles)) / math.sqrt(count)


def slot_index(slots, size_z):
    index_row = np.arange(slots)
    return np.where(2 * index_row < slots, index_row, index_row + size_z - slots)


def signed_np(values, count):
    return np.where(2 * values <= count, values, values - count)


def reach(cols, size_x, size_y):
    fx = signed_np(np.arange(size_x), size_x)
    fy = signed_np(np.arange(size_y), size_y)
    radius_sq = np.sort((fx[:, None] ** 2 + fy[None, :] ** 2).reshape(-1))
    return math.isqrt(int(radius_sq[cols - 1]))


def window(radius, size, step):
    return min(size, -(-(2 * radius + 1) // step) * step)


def signed_freq(values, count):
    return jnp.where(2 * values <= count, values, values - count)


def loop(count):
    return lambda step_fn: lax.fori_loop(0, count, step_fn, 0)


def plane_kernel(
    xw, yw, rows_ref, spread_ref, pot_ref, sy_ref, syt_ref, sx_ref, sxt_ref, out_ref, grid_ref, line_ref
):
    planes = pot_ref.shape[0]
    cols = spread_ref.shape[0]
    grid_ref[...] = jnp.zeros_like(grid_ref)

    @loop(cols // 32)
    def _(step, carry):
        base = pl.multiple_of(step * 32, 32)
        for i in range(32):
            grid_ref[pl.ds(rows_ref[base + i], 1), :] = spread_ref[pl.ds(base + i, 1), :]
        return carry

    for slot in range(xw):
        chunk = jnp.transpose(grid_ref[slot * yw : (slot + 1) * yw, :])
        for half in range(yw // 128):
            line_ref[half, pl.ds(slot, planes, stride=xw), :] = chunk[:planes, half * 128 : (half + 1) * 128]

    @loop(planes // 2)
    def _(step, carry):
        for i in range(2):
            plane = step * 2 + i
            at = pl.ds(pl.multiple_of(plane * xw, xw), xw)
            parts = [line_ref[half, at, :].astype(BF16) for half in range(yw // 128)]
            part = parts[0] if len(parts) == 1 else jnp.concatenate(parts, axis=1)
            lines = jnp.dot(part, sy_ref[...], preferred_element_type=F32).astype(BF16)
            field = jnp.dot(sx_ref[...], lines, preferred_element_type=F32)
            product = (field * (pot_ref[plane].astype(F32) - LEVEL)).astype(BF16)
            lines = jnp.dot(sxt_ref[...], product, preferred_element_type=F32).astype(BF16)
            back = jnp.dot(lines, syt_ref[...], preferred_element_type=F32)
            for half in range(yw // 128):
                line_ref[half, at, :] = back[:, half * 128 : (half + 1) * 128]
        return carry

    for slot in range(xw):
        parts = [line_ref[half, pl.ds(slot, planes, stride=xw), :] for half in range(yw // 128)]
        chunk = parts[0] if len(parts) == 1 else jnp.concatenate(parts, axis=1)
        if planes < 128:
            chunk = jnp.concatenate([chunk, jnp.zeros((128 - planes, yw), F32)], axis=0)
        grid_ref[slot * yw : (slot + 1) * yw, :] = jnp.transpose(chunk)

    @loop(cols // 32)
    def _(step, carry):
        base = pl.multiple_of(step * 32, 32)
        for i in range(32):
            out_ref[pl.ds(base + i, 1), :] = grid_ref[pl.ds(rows_ref[base + i], 1), :]
        return carry


def apply_planes(rows, spread, potential, xw, yw):
    planes, size_x, size_y = potential.shape
    cols = spread.shape[0]
    table_x = hartley(size_x)[:, (np.arange(xw) - xw // 2) % size_x]
    table_y = hartley(size_y)[:, (np.arange(yw) - yw // 2) % size_y]
    vmem = pl.BlockSpec(memory_space=pltpu.VMEM)
    cast = lambda a: jnp.asarray(a, BF16)
    return pl.pallas_call(
        functools.partial(plane_kernel, xw, yw),
        out_shape=jax.ShapeDtypeStruct((cols, 128), F32),
        in_specs=[pl.BlockSpec(memory_space=pltpu.SMEM)] + [vmem] * 6,
        out_specs=vmem,
        scratch_shapes=[
            pltpu.VMEM((xw * yw, 128), F32),
            pltpu.VMEM((yw // 128, planes * xw, 128), F32),
        ],
        compiler_params=pltpu.CompilerParams(vmem_limit_bytes=56 * 2**20),
    )(rows, spread, potential, cast(table_y.T), cast(table_y), cast(table_x), cast(table_x.T))


def body(coeffs, potential, stick_cells, block, rotation):
    col_count, slots = coeffs.shape[1:]
    planes, size_x, size_y = potential.shape
    groups = lax.axis_size("ga")
    cols = stick_cells.shape[0]
    size_z = planes * groups
    radius = reach(cols, size_x, size_y)
    xw = window(radius, size_x, 16)
    yw = window(radius, size_y, 128)
    slot_ids = slot_index(slots, size_z)
    table_z = hartley(size_z)[:, slot_ids]
    freq_x = signed_freq(stick_cells // size_y, size_x)
    freq_y = signed_freq(stick_cells % size_y, size_y)
    rows = (freq_x + xw // 2) * yw + freq_y + yw // 2

    mine = lax.axis_index("ga") * col_count
    local_x = lax.dynamic_slice_in_dim(freq_x, mine, col_count).astype(F32)
    local_y = lax.dynamic_slice_in_dim(freq_y, mine, col_count).astype(F32)
    plane_part = 0.5 * (
        (2.0 * math.pi / size_x) ** 2 * local_x * local_x
        + (2.0 * math.pi / size_y) ** 2 * local_y * local_y
    )
    freq_z = signed_np(slot_ids, size_z)
    line_part = jnp.asarray(0.5 * (2.0 * math.pi / size_z) ** 2 * freq_z * freq_z, F32)
    kinetic = plane_part[:, None] + line_part[None, :]

    table_f = jnp.asarray(table_z.reshape(groups, planes, slots), F32)
    table_b = jnp.asarray(table_z.reshape(groups, planes, slots), F32)
    high = lax.Precision.HIGH
    sent = jnp.einsum("sk,gzk->gsz", coeffs[0], table_f, precision=high).astype(BF16)
    spread = lax.all_to_all(sent, "ga", split_axis=0, concat_axis=0, tiled=True)
    spread = spread.reshape(cols, planes).astype(F32)
    spread = jnp.pad(spread, ((0, 0), (0, 128 - planes)))
    picked = apply_planes(rows, spread, potential, xw, yw)
    picked = picked[:, :planes].astype(BF16).reshape(groups, col_count, planes)
    returned = lax.all_to_all(picked, "ga", split_axis=0, concat_axis=0, tiled=True)
    results = (
        jnp.einsum("gsz,gzk->sk", returned.astype(F32), table_b, precision=high) + (kinetic + LEVEL) * coeffs[0]
    )
    panel = results.reshape(1, col_count * slots).astype(BF16)
    summed = jnp.dot(
        rotation,
        lax.all_gather(panel, "band", axis=0, tiled=True),
        preferred_element_type=F32,
    )
    rotated = (block.astype(F32) + summed).astype(BF16)
    return (results[None], rotated)


def solution(mesh):
    return jax.shard_map(
        body,
        mesh=mesh,
        in_specs=(
            P("band", "ga", None),
            P("ga", None, None),
            P(),
            P("band", "ga"),
            P("band", None),
        ),
        out_specs=(P("band", "ga", None), P("band", "ga")),
        check_vma=False,
    )
```

profile of v0, /device:TPU:0, one launch (start us, length us, event | category | flops | bytes accessed | tf_op | source)
XLA Modules:
  0.0 175.1 jit_solution(17095205755277456506)
XLA Ops:
  7.2 0.0 copy-start
  7.2 0.0 copy-start.4
  7.2 2.5 %fusion.4 = bf16[4,1024,64]{1,2,0:T(8,128)(2,1)} fusion(f32[4,64,128]{2,1,0:T(8,128)} %constant.72.clone, f32[1,1024,128]{2,1,0:T(8,128)} %param.12), kind=kOutput, calls=%fused_computation.7 | convolution fusion | flops 201588736 | bytes 1179648 | tf_op jit(solution)/shard_map/sk,gzk->gsz/dot_general | solution.py:150
  9.7 4.2 %all-to-all-start = ((bf16[4,1024,64]{1,2,0:T(8,128)(2,1)}), bf16[4,1024,64]{1,2,0:T(8,128)(2,1)S(1)}, u32[]{:S(2)}, u32[]{:S(2)}) async-start(bf16[4,1024,64]{1,2,0:T(8,128)(2,1)} %fusion.4), calls=%async_computation | async-start | bytes 1048576 | tf_op jit(solution)/shard_map/all_to_all | solution.py:151
  13.9 0.0 copy-done.4
  13.9 0.6 add_select_fusion.2
  14.6 8.2 %all-to-all-done = bf16[4,1024,64]{1,2,0:T(8,128)(2,1)S(1)} async-done(((bf16[4,1024,64]{1,2,0:T(8,128)(2,1)}), bf16[4,1024,64]{1,2,0:T(8,128)(2,1)S(1)}, u32[]{:S(2)}, u32[]{:S(2)}) %all-to-all-start) | async-done | bytes 524320 | tf_op jit(solution)/shard_map/all_to_all | solution.py:151
  22.8 0.5 copy.19
  23.3 1.5 pad_convert_fusion.spread_ref
  24.7 45.3 %shard_map.131 = f32[4096,128]{1,0:T(8,128)} custom-call(s32[4096]{0:T(1024)} %get-tuple-element.3.rows_ref, f32[4096,128]{1,0:T(8,128)} %pad_convert_fusion.spread_ref, bf16[64,256,256]{2,1,0:T(8,128)(2,1)} %pot_ref.1, bf16[128,256]{1,0:T(8,128)(2,1)} %constant.73.clone.sy_ref, bf16[256,128]{1,0:T(8,128)(2,1)} %constant.74.clone.syt_ref, ...), custom_call_target="tpu_custom_call" | custom-call | tf_op jit(solution)/shard_map/pallas_call | solution.py:108
  70.1 0.0 copy-start.1
  70.1 0.0 copy-start.3
  70.1 0.0 copy-start.5
  70.1 1.8 %slice.7 = bf16[4096,64]{1,0:T(8,128)(2,1)S(1)} slice(f32[4096,128]{1,0:T(8,128)} %shard_map.131), slice={[0:4096], [0:64]} | slice | bytes 1048576 | tf_op jit(solution)/shard_map/slice | solution.py:155
  71.8 1.2 copy.20
  73.0 0.0 copy-start.2
  73.0 3.6 %all-to-all-start.1 = ((bf16[4,1024,64]{1,2,0:T(8,128)(2,1)}), bf16[4,1024,64]{1,2,0:T(8,128)(2,1)S(1)}, u32[]{:S(2)}, u32[]{:S(2)}) async-start(bf16[4,1024,64]{1,2,0:T(8,128)(2,1)} %copy.20), calls=%async_computation.1 | async-start | bytes 1048576 | tf_op jit(solution)/shard_map/all_to_all | solution.py:156
  76.6 0.0 all-gather.3.cloned.1.call-start
  76.7 8.7 %all-to-all-done.1 = bf16[4,1024,64]{1,2,0:T(8,128)(2,1)S(1)} async-done(((bf16[4,1024,64]{1,2,0:T(8,128)(2,1)}), bf16[4,1024,64]{1,2,0:T(8,128)(2,1)S(1)}, u32[]{:S(2)}, u32[]{:S(2)}) %all-to-all-start.1) | async-done | bytes 524320 | tf_op jit(solution)/shard_map/all_to_all | solution.py:156
  85.4 0.0 copy-done.1
  85.4 0.0 copy-done.3
  85.4 0.0 copy-done.5
  85.4 1.4 fusion.11
  86.8 0.9 reshape.27
  87.7 0.0 all-gather.3.cloned.1.call-update
  87.7 74.5 %all-gather.3.cloned.1.call-done = bf16[8,1,131072]{2,1,0:T(2,128)(2,1)} async-done(((bf16[1,1,131072]{2,1,0:T(2,128)(2,1)}), bf16[8,1,131072]{2,1,0:T(2,128)(2,1)}) %all-gather.3.cloned.1.call-update) | async-done | bytes 2097168 | tf_op jit(solution)/shard_map/all_gather | solution.py:163
  162.2 0.0 copy-done
  162.2 0.0 copy-done.2
  162.2 6.0 %fusion.1 = bf16[8,131072]{1,0:T(8,128)(2,1)} fusion(bf16[8,8]{1,0:T(8,128)(2,1)S(1)} %copy-done, bf16[8,131072]{1,0:T(8,128)(2,1)S(1)} %copy-done.2, bf16[8,1,131072]{2,1,0:T(2,128)(2,1)} %all-gather.3.cloned.1.call-done), kind=kOutput, calls=%fused_computation.2 | convolution fusion | flops 19922944 | bytes 6291584 | tf_op jit(solution)/shard_map/dot_general | solution.py:161
  (1 shorter events, 0.0 us)
Async XLA Ops:
  7.2 155.1 %copy-start = (bf16[8,8]{1,0:T(8,128)(2,1)S(1)}, bf16[8,8]{1,0:T(8,128)(2,1)}, u32[]{:S(2)}) copy-start(bf16[8,8]{1,0:T(8,128)(2,1)} %param.16) | copy-start | bytes 388
  7.2 6.8 %copy-start.4 = (s32[4096]{0:T(1024)S(1)}, s32[4096]{0:T(1024)}, u32[]{:S(2)}) copy-start(s32[4096]{0:T(1024)} %param.14) | copy-start | bytes 49156
  9.7 13.1 %all-to-all-start = ((bf16[4,1024,64]{1,2,0:T(8,128)(2,1)}), bf16[4,1024,64]{1,2,0:T(8,128)(2,1)S(1)}, u32[]{:S(2)}, u32[]{:S(2)}) async-start(bf16[4,1024,64]{1,2,0:T(8,128)(2,1)} %fusion.4), calls=%async_computation | async-start | bytes 1048576 | tf_op jit(solution)/shard_map/all_to_all | solution.py:151
  70.1 15.4 %copy-start.1 = (f32[1,1024,128]{2,1,0:T(8,128)S(1)}, f32[1,1024,128]{2,1,0:T(8,128)}, u32[]{:S(2)}) copy-start(f32[1,1024,128]{2,1,0:T(8,128)} %param.12) | copy-start | bytes 1572868
  70.1 15.4 %copy-start.3 = (f32[4,64,128]{2,1,0:T(8,128)S(1)}, f32[4,64,128]{2,1,0:T(8,128)}, u32[]{:S(2)}) copy-start(f32[4,64,128]{2,1,0:T(8,128)} %constant.72.clone) | copy-start | bytes 393220
  70.1 15.4 %copy-start.5 = (f32[128]{0:T(128)S(1)}, f32[128]{0:T(128)}, u32[]{:S(2)}) copy-start(f32[128]{0:T(128)} %constant.71.clone) | copy-start | bytes 1540
  73.0 89.3 %copy-start.2 = (bf16[8,131072]{1,0:T(8,128)(2,1)S(1)}, bf16[8,131072]{1,0:T(8,128)(2,1)}, u32[]{:S(2)}) copy-start(bf16[8,131072]{1,0:T(8,128)(2,1)} %param.15) | copy-start | bytes 6291460
  73.0 12.4 %all-to-all-start.1 = ((bf16[4,1024,64]{1,2,0:T(8,128)(2,1)}), bf16[4,1024,64]{1,2,0:T(8,128)(2,1)S(1)}, u32[]{:S(2)}, u32[]{:S(2)}) async-start(bf16[4,1024,64]{1,2,0:T(8,128)(2,1)} %copy.20), calls=%async_computation.1 | async-start | bytes 1048576 | tf_op jit(solution)/shard_map/all_to_all | solution.py:156
  76.6 85.6 %all-gather.3.cloned.1.call-start = ((), (), s32[]{:S(2)}) async-start(), calls=%async_computation.2 | async-start | bytes 4718592 | tf_op jit(solution)/shard_map/all_gather | solution.py:163
Sparse Core Ops, SparseCore 0:
  87.9 74.3 all-gather.2
where the time goes:
time: 175 us
  waiting for transfers between devices  91.5 us (52%)
  Pallas kernels  45.3 us (26%)
  between operations  14.1 us (8%)
  matrix products  9.93 us (6%)
  starting transfers between devices  7.88 us (5%)
  local copies, waits for them, and re-layouts  4.32 us (2%)
  other arithmetic  2.1 us (1%)
    all_gather x1, waiting for transfers between devices, body(): lax.all_gather(panel, 'band', axis=0, tiled=True)  74.5 us
    pallas_call x1, Pallas kernels, apply_planes(): pl.pallas_call(functools.partial(plane_kernel, xw, yw), out_shape=jax.Sha...  45.3 us
    all_to_all x1, waiting for transfers between devices, body(): lax.all_to_all(picked, 'ga', split_axis=0, concat_axis=0, tiled=True)  8.74 us
    all_to_all x1, waiting for transfers between devices, body(): spread = lax.all_to_all(sent, 'ga', split_axis=0, concat_axis=0, tiled=True)  8.22 us
    dot_general x1, matrix products, body(): jnp.dot(rotation, lax.all_gather(panel, 'band', axis=0, tiled=True), pref...  6.03 us
    all_to_all x1, starting transfers between devices, body(): spread = lax.all_to_all(sent, 'ga', split_axis=0, concat_axis=0, tiled=True)  4.24 us
    all_to_all x1, starting transfers between devices, body(): lax.all_to_all(picked, 'ga', split_axis=0, concat_axis=0, tiled=True)  3.6 us
  transfers between devices with their start and end apart: 3, of which 3 were waited for; matrix products, arithmetic and copies ran while one was open for 0% of the time, Pallas kernels for 0%

commit v1 on v0

--- a/solution.py
+++ b/solution.py
@@ -49,17 +49,18 @@
 
 
 def plane_kernel(
-    xw, yw, rows_ref, spread_ref, pot_ref, sy_ref, syt_ref, sx_ref, sxt_ref, out_ref, grid_ref, line_ref
+    xw, yw, rows_ref, spread_ref, pot_ref, sy_ref, syt_ref, sx_ref, sxt_ref, out_ref, cols_ref, grid_ref, line_ref
 ):
     planes = pot_ref.shape[0]
     cols = spread_ref.shape[0]
     grid_ref[...] = jnp.zeros_like(grid_ref)
+    cols_ref[:, :planes] = spread_ref[...].astype(F32)
 
     @loop(cols // 32)
     def _(step, carry):
         base = pl.multiple_of(step * 32, 32)
         for i in range(32):
-            grid_ref[pl.ds(rows_ref[base + i], 1), :] = spread_ref[pl.ds(base + i, 1), :]
+            grid_ref[pl.ds(rows_ref[base + i], 1), :] = cols_ref[pl.ds(base + i, 1), :]
         return carry
 
     for slot in range(xw):
@@ -94,8 +95,10 @@
     def _(step, carry):
         base = pl.multiple_of(step * 32, 32)
         for i in range(32):
-            out_ref[pl.ds(base + i, 1), :] = grid_ref[pl.ds(rows_ref[base + i], 1), :]
+            cols_ref[pl.ds(base + i, 1), :] = grid_ref[pl.ds(rows_ref[base + i], 1), :]
         return carry
+
+    out_ref[...] = cols_ref[:, :planes].astype(BF16)
 
 
 def apply_planes(rows, spread, potential, xw, yw):
@@ -107,15 +110,149 @@
     cast = lambda a: jnp.asarray(a, BF16)
     return pl.pallas_call(
         functools.partial(plane_kernel, xw, yw),
-        out_shape=jax.ShapeDtypeStruct((cols, 128), F32),
+        out_shape=jax.ShapeDtypeStruct((cols, planes), BF16),
         in_specs=[pl.BlockSpec(memory_space=pltpu.SMEM)] + [vmem] * 6,
         out_specs=vmem,
         scratch_shapes=[
+            pltpu.VMEM((cols, 128), F32),
             pltpu.VMEM((xw * yw, 128), F32),
             pltpu.VMEM((yw // 128, planes * xw, 128), F32),
         ],
         compiler_params=pltpu.CompilerParams(vmem_limit_bytes=56 * 2**20),
     )(rows, spread, potential, cast(table_y.T), cast(table_y), cast(table_x), cast(table_x.T))
+
+
+def gather_kernel(
+    depth, width, pieces, own_ref, out_ref, own_sem, line_send, line_recv, cross_send, cross_recv
+):
+    band = lax.axis_index("band")
+    z = band // width
+    x = band % width
+    rows = own_ref.shape[0] // pieces
+    ways = (1, -1)
+
+    def inside(at):
+        return jnp.logical_and(at >= 0, at < depth)
+
+    def source(d, slot, cut):
+        return own_ref.at[cut, :] if d == 0 else out_ref.at[slot, cut, :]
+
+    def line_copy(way, d, piece):
+        cut = pl.ds(piece * rows, rows)
+        slot = (z - ways[way] * d) * width + x
+        return pltpu.make_async_remote_copy(
+            src_ref=source(d, slot, cut),
+            dst_ref=out_ref.at[slot, cut, :],
+            send_sem=line_send.at[way, d, piece],
+            recv_sem=line_recv.at[way, d, piece],
+            device_id={"band": (z + ways[way]) * width + x},
+            device_id_type=pl.DeviceIdType.MESH,
+        )
+
+    def cross_copy(hop, way, d, piece):
+        cut = pl.ds(piece * rows, rows)
+        slot = (z - ways[way] * d) * width + x
+        return pltpu.make_async_remote_copy(
+            src_ref=source(d, slot, cut),
+            dst_ref=out_ref.at[slot, cut, :],
+            send_sem=cross_send.at[hop - 1, way, d, piece],
+            recv_sem=cross_recv.at[hop - 1, way, d, piece],
+            device_id={"band": z * width + (x + hop) % width},
+            device_id_type=pl.DeviceIdType.MESH,
+        )
+
+    def line_arrival(way, d, piece):
+        cut = pl.ds(piece * rows, rows)
+        slot = (z - ways[way] * d) * width + x
+        return pltpu.make_async_copy(
+            out_ref.at[slot, cut, :], out_ref.at[slot, cut, :], line_recv.at[way, d - 1, piece]
+        )
+
+    def cross_arrival(hop, way, d, piece):
+        cut = pl.ds(piece * rows, rows)
+        slot = (z - ways[way] * d) * width + (x + width - hop) % width
+        return pltpu.make_async_copy(
+            out_ref.at[slot, cut, :], out_ref.at[slot, cut, :], cross_recv.at[hop - 1, way, d, piece]
+        )
+
+    barrier = pltpu.get_barrier_semaphore()
+    for way in ways:
+
+        @pl.when(inside(z + way))
+        def _(way=way):
+            pl.semaphore_signal(
+                barrier,
+                inc=1,
+                device_id={"band": (z + way) * width + x},
+                device_id_type=pl.DeviceIdType.MESH,
+            )
+
+    for hop in range(1, width):
+        pl.semaphore_signal(
+            barrier,
+            inc=1,
+            device_id={"band": z * width + (x + hop) % width},
+            device_id_type=pl.DeviceIdType.MESH,
+        )
+    beside = jnp.where(z > 0, 1, 0) + jnp.where(z < depth - 1, 1, 0)
+    pl.semaphore_wait(barrier, beside + width - 1)
+
+    own = pltpu.make_async_copy(own_ref, out_ref.at[band], own_sem)
+    own.start()
+
+    for d in range(depth):
+        for piece in range(pieces):
+            for way in range(2):
+
+                @pl.when(inside(z - ways[way] * d))
+                def _(way=way):
+                    if d > 0:
+                        line_arrival(way, d, piece).wait()
+
+                    if d < depth - 1:
+
+                        @pl.when(inside(z + ways[way]))
+                        def _():
+                            line_copy(way, d, piece).start()
+
+                    if d > 0 or way == 0:
+                        for hop in range(1, width):
+                            cross_copy(hop, way, d, piece).start()
+
+    own.wait()
+    for d in range(depth):
+        for piece in range(pieces):
+            for way in range(2):
+
+                @pl.when(inside(z - ways[way] * d))
+                def _(way=way):
+                    if d < depth - 1:
+
+                        @pl.when(inside(z + ways[way]))
+                        def _():
+                            line_copy(way, d, piece).wait_send()
+
+                    if d > 0 or way == 0:
+                        for hop in range(1, width):
+                            cross_copy(hop, way, d, piece).wait_send()
+                            cross_arrival(hop, way, d, piece).wait()
+
+
+def gather_panel(own, bands):
+    width = bands // 4 if bands % 4 == 0 and bands > 4 else 1
+    depth = bands // width
+    pieces = 2
+    line = pltpu.SemaphoreType.DMA((2, depth, pieces))
+    cross = pltpu.SemaphoreType.DMA((max(width - 1, 1), 2, depth, pieces))
+    anywhere = pl.BlockSpec(memory_space=pl.ANY)
+    return pl.pallas_call(
+        functools.partial(gather_kernel, depth, width, pieces),
+        out_shape=jax.ShapeDtypeStruct((bands,) + own.shape, own.dtype),
+        in_specs=[anywhere],
+        out_specs=anywhere,
+        scratch_shapes=[pltpu.SemaphoreType.DMA, line, line, cross, cross],
+        compiler_params=pltpu.CompilerParams(collective_id=0, has_side_effects=True),
+    )(own)
 
 
 def body(coeffs, potential, stick_cells, block, rotation):
@@ -149,18 +286,17 @@
     high = lax.Precision.HIGH
     sent = jnp.einsum("sk,gzk->gsz", coeffs[0], table_f, precision=high).astype(BF16)
     spread = lax.all_to_all(sent, "ga", split_axis=0, concat_axis=0, tiled=True)
-    spread = spread.reshape(cols, planes).astype(F32)
-    spread = jnp.pad(spread, ((0, 0), (0, 128 - planes)))
+    spread = spread.reshape(cols, planes)
     picked = apply_planes(rows, spread, potential, xw, yw)
-    picked = picked[:, :planes].astype(BF16).reshape(groups, col_count, planes)
+    picked = picked.reshape(groups, col_count, planes)
     returned = lax.all_to_all(picked, "ga", split_axis=0, concat_axis=0, tiled=True)
     results = (
         jnp.einsum("gsz,gzk->sk", returned.astype(F32), table_b, precision=high) + (kinetic + LEVEL) * coeffs[0]
     )
-    panel = results.reshape(1, col_count * slots).astype(BF16)
+    panel = gather_panel(results.astype(BF16), lax.axis_size("band"))
     summed = jnp.dot(
         rotation,
-        lax.all_gather(panel, "band", axis=0, tiled=True),
+        panel.reshape(panel.shape[0], col_count * slots),
         preferred_element_type=F32,
     )
     rotated = (block.astype(F32) + summed).astype(BF16)

time: 175 us -> 111 us (0.63)
  waiting for transfers between devices: 91.5 us -> 17 us
  Pallas kernels: 45.3 us -> 72.3 us
  between operations: 14.1 us -> 0.71 us
    all_gather x1 -> x0, waiting for transfers between devices: 74.5 us -> none  [body(): lax.all_gather(panel, 'band', axis=0, tiled=True)]
    pallas_call x0 -> x1, Pallas kernels: none -> 27.4 us  [gather_panel(): pl.pallas_call(functools.partial(gather_kernel, depth, width, pieces), ou...]
    slice x1 -> x0, local copies, waits for them, and re-layouts: 1.76 us -> none  [body(): picked = picked[:, :planes].astype(BF16).reshape(groups, col_count, planes)]
  transfers between devices with their start and end apart: 3 -> 2, of which waited for: 3 -> 2; matrix products, arithmetic and copies ran while one was open for 0% -> 1% of each run, Pallas kernels for 0% -> 0%
where the time goes in v1:
time: 111 us; the launch traced here: 110 us
  Pallas kernels  72.3 us (65%)
  waiting for transfers between devices  17 us (15%)
  matrix products  8.31 us (7%)
  starting transfers between devices  7.71 us (7%)
  local copies, waits for them, and re-layouts  3.75 us (3%)
    pallas_call x1, Pallas kernels, apply_planes(): pl.pallas_call(functools.partial(plane_kernel, xw, yw), out_shape=jax.Sha...  44.8 us
    pallas_call x1, Pallas kernels, gather_panel(): pl.pallas_call(functools.partial(gather_kernel, depth, width, pieces), ou...  27.4 us
    all_to_all x1, waiting for transfers between devices, body(): lax.all_to_all(picked, 'ga', split_axis=0, concat_axis=0, tiled=True)  8.77 us
    all_to_all x1, waiting for transfers between devices, body(): spread = lax.all_to_all(sent, 'ga', split_axis=0, concat_axis=0, tiled=True)  8.22 us
    dot_general x1, matrix products, body(): jnp.dot(rotation, panel.reshape(panel.shape[0], col_count * slots), prefe...  4.32 us
    all_to_all x1, starting transfers between devices, body(): spread = lax.all_to_all(sent, 'ga', split_axis=0, concat_axis=0, tiled=True)  4.24 us
    all_to_all x1, starting transfers between devices, body(): lax.all_to_all(picked, 'ga', split_axis=0, concat_axis=0, tiled=True)  3.47 us
    dot_general x1, matrix products, body(): jnp.einsum('sk,gzk->gsz', coeffs[0], table_f, precision=high).astype(BF16)  2.5 us
  transfers between devices with their start and end apart: 2, of which 2 were waited for; matrix products, arithmetic and copies ran while one was open for 1% of the time, Pallas kernels for 0%

profile of v1, /device:TPU:0, one launch (start us, length us, event | category | flops | bytes accessed | tf_op | source)
XLA Modules:
  0.0 110.4 jit_solution(4893672372647260909)
XLA Ops:
  0.6 0.0 copy-start
  0.6 0.0 copy-start.4
  0.7 2.5 %fusion.4 = bf16[4,1024,64]{1,2,0:T(8,128)(2,1)} fusion(f32[4,64,128]{2,1,0:T(8,128)} %constant.69.clone, f32[1,1024,128]{2,1,0:T(8,128)} %param.12), kind=kOutput, calls=%fused_computation.6 | convolution fusion | flops 201588736 | bytes 1179648 | tf_op jit(solution)/shard_map/sk,gzk->gsz/dot_general | solution.py:287
  3.2 4.2 %all-to-all-start = ((bf16[4,1024,64]{1,2,0:T(8,128)(2,1)}), bf16[4,1024,64]{1,2,0:T(8,128)(2,1)S(1)}, u32[]{:S(2)}, u32[]{:S(2)}) async-start(bf16[4,1024,64]{1,2,0:T(8,128)(2,1)} %fusion.4), calls=%async_computation | async-start | bytes 1048576 | tf_op jit(solution)/shard_map/all_to_all | solution.py:288
  7.4 0.0 copy-done.4
  7.4 0.6 add_select_fusion.2
  8.0 8.2 %all-to-all-done = bf16[4,1024,64]{1,2,0:T(8,128)(2,1)S(1)} async-done(((bf16[4,1024,64]{1,2,0:T(8,128)(2,1)}), bf16[4,1024,64]{1,2,0:T(8,128)(2,1)S(1)}, u32[]{:S(2)}, u32[]{:S(2)}) %all-to-all-start) | async-done | bytes 524320 | tf_op jit(solution)/shard_map/all_to_all | solution.py:288
  16.2 1.3 %copy.14 = bf16[4,1024,64]{2,1,0:T(8,128)(2,1)} copy(bf16[4,1024,64]{1,2,0:T(8,128)(2,1)S(1)} %all-to-all-done) | data formatting | bytes 1048576 | tf_op jit(solution)/shard_map/all_to_all | solution.py:288
  17.6 44.8 %shard_map.131 = bf16[4096,64]{1,0:T(8,128)(2,1)} custom-call(s32[4096]{0:T(1024)} %get-tuple-element.3.rows_ref, bf16[4096,64]{1,0:T(8,128)(2,1)} %bitcast.31, bf16[64,256,256]{2,1,0:T(8,128)(2,1)} %pot_ref.1, bf16[128,256]{1,0:T(8,128)(2,1)} %constant.70.clone.sy_ref, bf16[256,128]{1,0:T(8,128)(2,1)} %constant.71.clone.syt_ref, ...), custom_call_target="tpu_custom_call" | custom-call | tf_op jit(solution)/shard_map/pallas_call | solution.py:111
  62.4 0.0 copy-start.1
  62.4 0.0 copy-start.3
  62.4 0.0 copy-start.5
  62.4 2.4 %copy.15 = bf16[4,1024,64]{1,2,0:T(8,128)(2,1)} copy(bf16[4,1024,64]{2,1,0:T(8,128)(2,1)} %bitcast.32) | data formatting | bytes 1048576 | tf_op jit(solution)/shard_map/reshape | solution.py:291
  64.8 3.5 %all-to-all-start.1 = ((bf16[4,1024,64]{1,2,0:T(8,128)(2,1)}), bf16[4,1024,64]{1,2,0:T(8,128)(2,1)S(1)}, u32[]{:S(2)}, u32[]{:S(2)}) async-start(bf16[4,1024,64]{1,2,0:T(8,128)(2,1)} %copy.15), calls=%async_computation.1 | async-start | bytes 1048576 | tf_op jit(solution)/shard_map/all_to_all | solution.py:292
  68.3 0.0 copy-start.2
  68.3 8.8 %all-to-all-done.1 = bf16[4,1024,64]{1,2,0:T(8,128)(2,1)S(1)} async-done(((bf16[4,1024,64]{1,2,0:T(8,128)(2,1)}), bf16[4,1024,64]{1,2,0:T(8,128)(2,1)S(1)}, u32[]{:S(2)}, u32[]{:S(2)}) %all-to-all-start.1) | async-done | bytes 524320 | tf_op jit(solution)/shard_map/all_to_all | solution.py:292
  77.1 0.0 copy-done.1
  77.1 0.0 copy-done.3
  77.1 0.0 copy-done.5
  77.1 1.5 %fusion.11 = (bf16[1024,128]{1,0:T(8,128)(2,1)}, f32[1024,128]{1,0:T(8,128)}) fusion(f32[1,1024,128]{2,1,0:T(8,128)S(1)} %copy-done.1, f32[128]{0:T(128)S(1)} %copy-done.5, f32[1024]{0:T(1024)S(1)} %fusion.10, bf16[4,1024,64]{1,2,0:T(8,128)(2,1)S(1)} %all-to-all-done.1, f32[4,64,128]{2,1,0:T(8,128)S(1)} %copy-done.3), kind=kOutput, calls=%fused_computation.28 | convolution fusion | flops 201981952 | bytes 1970688 | tf_op jit(solution)/shard_map/gsz,gzk->sk/dot_general | solution.py:294
  78.6 27.4 %shard_map.132 = bf16[8,1024,128]{2,1,0:T(8,128)(2,1)} custom-call(bf16[1024,128]{1,0:T(8,128)(2,1)} %get-tuple-element.5.own_ref), custom_call_target="tpu_custom_call" | custom-call | tf_op jit(solution)/shard_map/pallas_call | solution.py:248
  106.0 0.0 copy-done
  106.1 0.0 copy-done.2
  106.1 4.3 %fusion.1 = bf16[8,131072]{1,0:T(8,128)(2,1)} fusion(bf16[8,8]{1,0:T(8,128)(2,1)S(1)} %copy-done, bf16[8,131072]{1,0:T(8,128)(2,1)S(1)} %copy-done.2, bf16[1,8,1024,128]{3,2,1,0:T(8,128)(2,1)} %bitcast.30), kind=kOutput, calls=%fused_computation.2 | convolution fusion | flops 19922944 | bytes 6291584 | tf_op jit(solution)/shard_map/dot_general | solution.py:297
  (1 shorter events, 0.0 us)
Async XLA Ops:
  0.6 105.4 %copy-start = (bf16[8,8]{1,0:T(8,128)(2,1)S(1)}, bf16[8,8]{1,0:T(8,128)(2,1)}, u32[]{:S(2)}) copy-start(bf16[8,8]{1,0:T(8,128)(2,1)} %param.16) | copy-start | bytes 388
  0.6 6.8 %copy-start.4 = (s32[4096]{0:T(1024)S(1)}, s32[4096]{0:T(1024)}, u32[]{:S(2)}) copy-start(s32[4096]{0:T(1024)} %param.14) | copy-start | bytes 49156
  3.2 13.1 %all-to-all-start = ((bf16[4,1024,64]{1,2,0:T(8,128)(2,1)}), bf16[4,1024,64]{1,2,0:T(8,128)(2,1)S(1)}, u32[]{:S(2)}, u32[]{:S(2)}) async-start(bf16[4,1024,64]{1,2,0:T(8,128)(2,1)} %fusion.4), calls=%async_computation | async-start | bytes 1048576 | tf_op jit(solution)/shard_map/all_to_all | solution.py:288
  62.4 14.7 %copy-start.1 = (f32[1,1024,128]{2,1,0:T(8,128)S(1)}, f32[1,1024,128]{2,1,0:T(8,128)}, u32[]{:S(2)}) copy-start(f32[1,1024,128]{2,1,0:T(8,128)} %param.12) | copy-start | bytes 1572868
  62.4 14.7 %copy-start.3 = (f32[4,64,128]{2,1,0:T(8,128)S(1)}, f32[4,64,128]{2,1,0:T(8,128)}, u32[]{:S(2)}) copy-start(f32[4,64,128]{2,1,0:T(8,128)} %constant.69.clone) | copy-start | bytes 393220
  62.4 14.7 %copy-start.5 = (f32[128]{0:T(128)S(1)}, f32[128]{0:T(128)}, u32[]{:S(2)}) copy-start(f32[128]{0:T(128)} %constant.68.clone) | copy-start | bytes 1540
  64.8 12.3 %all-to-all-start.1 = ((bf16[4,1024,64]{1,2,0:T(8,128)(2,1)}), bf16[4,1024,64]{1,2,0:T(8,128)(2,1)S(1)}, u32[]{:S(2)}, u32[]{:S(2)}) async-start(bf16[4,1024,64]{1,2,0:T(8,128)(2,1)} %copy.15), calls=%async_computation.1 | async-start | bytes 1048576 | tf_op jit(solution)/shard_map/all_to_all | solution.py:292
  68.3 37.7 %copy-start.2 = (bf16[8,131072]{1,0:T(8,128)(2,1)S(1)}, bf16[8,131072]{1,0:T(8,128)(2,1)}, u32[]{:S(2)}) copy-start(bf16[8,131072]{1,0:T(8,128)(2,1)} %param.15) | copy-start | bytes 6291460

commit v2 on v1

--- a/solution.py
+++ b/solution.py
@@ -12,6 +12,7 @@
 BF16 = jnp.bfloat16
 F32 = jnp.float32
 LEVEL = -0.5
+BATCH = 8
 
 
 def hartley(count):
@@ -68,20 +69,23 @@
         for half in range(yw // 128):
             line_ref[half, pl.ds(slot, planes, stride=xw), :] = chunk[:planes, half * 128 : (half + 1) * 128]
 
-    @loop(planes // 2)
+    @loop(planes // BATCH)
     def _(step, carry):
-        for i in range(2):
-            plane = step * 2 + i
-            at = pl.ds(pl.multiple_of(plane * xw, xw), xw)
-            parts = [line_ref[half, at, :].astype(BF16) for half in range(yw // 128)]
-            part = parts[0] if len(parts) == 1 else jnp.concatenate(parts, axis=1)
-            lines = jnp.dot(part, sy_ref[...], preferred_element_type=F32).astype(BF16)
-            field = jnp.dot(sx_ref[...], lines, preferred_element_type=F32)
-            product = (field * (pot_ref[plane].astype(F32) - LEVEL)).astype(BF16)
-            lines = jnp.dot(sxt_ref[...], product, preferred_element_type=F32).astype(BF16)
-            back = jnp.dot(lines, syt_ref[...], preferred_element_type=F32)
-            for half in range(yw // 128):
-                line_ref[half, at, :] = back[:, half * 128 : (half + 1) * 128]
+        ats = [pl.ds(pl.multiple_of((step * BATCH + i) * xw, xw), xw) for i in range(BATCH)]
+        halves = range(yw // 128)
+        def join(parts):
+            return parts[0] if len(parts) == 1 else jnp.concatenate(parts, axis=1)
+        part = jnp.concatenate([join([line_ref[h, at, :].astype(BF16) for h in halves]) for at in ats], axis=0)
+        lines = jnp.dot(part, sy_ref[...], preferred_element_type=F32).astype(BF16)
+        low = []
+        for i in range(BATCH):
+            field = jnp.dot(sx_ref[...], lines[i * xw : (i + 1) * xw], preferred_element_type=F32)
+            product = (field * (pot_ref[step * BATCH + i].astype(F32) - LEVEL)).astype(BF16)
+            low.append(jnp.dot(sxt_ref[...], product, preferred_element_type=F32).astype(BF16))
+        back = jnp.dot(jnp.concatenate(low, axis=0), syt_ref[...], preferred_element_type=F32)
+        for i, at in enumerate(ats):
+            for h in halves:
+                line_ref[h, at, :] = back[i * xw : (i + 1) * xw, h * 128 : (h + 1) * 128]
         return carry
 
     for slot in range(xw):

time: 111 us -> 97.1 us (0.87)
  Pallas kernels: 72.3 us -> 58.7 us
    pallas_call x1, Pallas kernels: 44.8 us -> 31.3 us  [apply_planes(): pl.pallas_call(functools.partial(plane_kernel, xw, yw), out_shape=jax.Sha...]
where the time goes in v2:
time: 97.1 us; the launch traced here: 96.8 us
  Pallas kernels  58.7 us (60%)
  waiting for transfers between devices  17 us (18%)
  matrix products  8.31 us (9%)
  starting transfers between devices  7.71 us (8%)
  local copies, waits for them, and re-layouts  3.75 us (4%)
    pallas_call x1, Pallas kernels, apply_planes(): pl.pallas_call(functools.partial(plane_kernel, xw, yw), out_shape=jax.Sha...  31.3 us
    pallas_call x1, Pallas kernels, gather_panel(): pl.pallas_call(functools.partial(gather_kernel, depth, width, pieces), ou...  27.4 us
    all_to_all x1, waiting for transfers between devices, body(): lax.all_to_all(picked, 'ga', split_axis=0, concat_axis=0, tiled=True)  8.77 us
    all_to_all x1, waiting for transfers between devices, body(): spread = lax.all_to_all(sent, 'ga', split_axis=0, concat_axis=0, tiled=True)  8.22 us
    dot_general x1, matrix products, body(): jnp.dot(rotation, panel.reshape(panel.shape[0], col_count * slots), prefe...  4.32 us
    all_to_all x1, starting transfers between devices, body(): spread = lax.all_to_all(sent, 'ga', split_axis=0, concat_axis=0, tiled=True)  4.24 us
    all_to_all x1, starting transfers between devices, body(): lax.all_to_all(picked, 'ga', split_axis=0, concat_axis=0, tiled=True)  3.47 us
    dot_general x1, matrix products, body(): jnp.einsum('sk,gzk->gsz', coeffs[0], table_f, precision=high).astype(BF16)  2.5 us
  transfers between devices with their start and end apart: 2, of which 2 were waited for; matrix products, arithmetic and copies ran while one was open for 1% of the time, Pallas kernels for 0%

profile of v2, /device:TPU:0, one launch (start us, length us, event | category | flops | bytes accessed | tf_op | source)
XLA Modules:
  0.0 96.8 jit_solution(6315866501754127353)
XLA Ops:
  0.6 0.0 copy-start
  0.6 0.0 copy-start.4
  0.7 2.5 %fusion.4 = bf16[4,1024,64]{1,2,0:T(8,128)(2,1)} fusion(f32[4,64,128]{2,1,0:T(8,128)} %constant.69.clone, f32[1,1024,128]{2,1,0:T(8,128)} %param.12), kind=kOutput, calls=%fused_computation.6 | convolution fusion | flops 201588736 | bytes 1179648 | tf_op jit(solution)/shard_map/sk,gzk->gsz/dot_general | solution.py:291
  3.2 4.2 %all-to-all-start = ((bf16[4,1024,64]{1,2,0:T(8,128)(2,1)}), bf16[4,1024,64]{1,2,0:T(8,128)(2,1)S(1)}, u32[]{:S(2)}, u32[]{:S(2)}) async-start(bf16[4,1024,64]{1,2,0:T(8,128)(2,1)} %fusion.4), calls=%async_computation | async-start | bytes 1048576 | tf_op jit(solution)/shard_map/all_to_all | solution.py:292
  7.4 0.0 copy-done.4
  7.4 0.6 add_select_fusion.2
  8.0 8.2 %all-to-all-done = bf16[4,1024,64]{1,2,0:T(8,128)(2,1)S(1)} async-done(((bf16[4,1024,64]{1,2,0:T(8,128)(2,1)}), bf16[4,1024,64]{1,2,0:T(8,128)(2,1)S(1)}, u32[]{:S(2)}, u32[]{:S(2)}) %all-to-all-start) | async-done | bytes 524320 | tf_op jit(solution)/shard_map/all_to_all | solution.py:292
  16.2 1.3 %copy.14 = bf16[4,1024,64]{2,1,0:T(8,128)(2,1)} copy(bf16[4,1024,64]{1,2,0:T(8,128)(2,1)S(1)} %all-to-all-done) | data formatting | bytes 1048576 | tf_op jit(solution)/shard_map/all_to_all | solution.py:292
  17.6 31.3 %shard_map.131 = bf16[4096,64]{1,0:T(8,128)(2,1)} custom-call(s32[4096]{0:T(1024)} %get-tuple-element.3.rows_ref, bf16[4096,64]{1,0:T(8,128)(2,1)} %bitcast.31, bf16[64,256,256]{2,1,0:T(8,128)(2,1)} %pot_ref.1, bf16[128,256]{1,0:T(8,128)(2,1)} %constant.70.clone.sy_ref, bf16[256,128]{1,0:T(8,128)(2,1)} %constant.71.clone.syt_ref, ...), custom_call_target="tpu_custom_call" | custom-call | tf_op jit(solution)/shard_map/pallas_call | solution.py:115
  48.8 0.0 copy-start.1
  48.8 0.0 copy-start.3
  48.8 0.0 copy-start.5
  48.9 2.4 %copy.15 = bf16[4,1024,64]{1,2,0:T(8,128)(2,1)} copy(bf16[4,1024,64]{2,1,0:T(8,128)(2,1)} %bitcast.32) | data formatting | bytes 1048576 | tf_op jit(solution)/shard_map/reshape | solution.py:295
  51.3 3.5 %all-to-all-start.1 = ((bf16[4,1024,64]{1,2,0:T(8,128)(2,1)}), bf16[4,1024,64]{1,2,0:T(8,128)(2,1)S(1)}, u32[]{:S(2)}, u32[]{:S(2)}) async-start(bf16[4,1024,64]{1,2,0:T(8,128)(2,1)} %copy.15), calls=%async_computation.1 | async-start | bytes 1048576 | tf_op jit(solution)/shard_map/all_to_all | solution.py:296
  54.8 0.0 copy-start.2
  54.8 8.8 %all-to-all-done.1 = bf16[4,1024,64]{1,2,0:T(8,128)(2,1)S(1)} async-done(((bf16[4,1024,64]{1,2,0:T(8,128)(2,1)}), bf16[4,1024,64]{1,2,0:T(8,128)(2,1)S(1)}, u32[]{:S(2)}, u32[]{:S(2)}) %all-to-all-start.1) | async-done | bytes 524320 | tf_op jit(solution)/shard_map/all_to_all | solution.py:296
  63.6 0.0 copy-done.1
  63.6 0.0 copy-done.3
  63.6 0.0 copy-done.5
  63.6 1.5 %fusion.11 = (bf16[1024,128]{1,0:T(8,128)(2,1)}, f32[1024,128]{1,0:T(8,128)}) fusion(f32[1,1024,128]{2,1,0:T(8,128)S(1)} %copy-done.1, f32[128]{0:T(128)S(1)} %copy-done.5, f32[1024]{0:T(1024)S(1)} %fusion.10, bf16[4,1024,64]{1,2,0:T(8,128)(2,1)S(1)} %all-to-all-done.1, f32[4,64,128]{2,1,0:T(8,128)S(1)} %copy-done.3), kind=kOutput, calls=%fused_computation.28 | convolution fusion | flops 201981952 | bytes 1970688 | tf_op jit(solution)/shard_map/gsz,gzk->sk/dot_general | solution.py:298
  65.0 27.4 %shard_map.132 = bf16[8,1024,128]{2,1,0:T(8,128)(2,1)} custom-call(bf16[1024,128]{1,0:T(8,128)(2,1)} %get-tuple-element.5.own_ref), custom_call_target="tpu_custom_call" | custom-call | tf_op jit(solution)/shard_map/pallas_call | solution.py:252
  92.5 0.0 copy-done
  92.5 0.0 copy-done.2
  92.5 4.3 %fusion.1 = bf16[8,131072]{1,0:T(8,128)(2,1)} fusion(bf16[8,8]{1,0:T(8,128)(2,1)S(1)} %copy-done, bf16[8,131072]{1,0:T(8,128)(2,1)S(1)} %copy-done.2, bf16[1,8,1024,128]{3,2,1,0:T(8,128)(2,1)} %bitcast.30), kind=kOutput, calls=%fused_computation.2 | convolution fusion | flops 19922944 | bytes 6291584 | tf_op jit(solution)/shard_map/dot_general | solution.py:301
  (1 shorter events, 0.0 us)
Async XLA Ops:
  0.6 91.9 %copy-start = (bf16[8,8]{1,0:T(8,128)(2,1)S(1)}, bf16[8,8]{1,0:T(8,128)(2,1)}, u32[]{:S(2)}) copy-start(bf16[8,8]{1,0:T(8,128)(2,1)} %param.16) | copy-start | bytes 388
  0.6 6.8 %copy-start.4 = (s32[4096]{0:T(1024)S(1)}, s32[4096]{0:T(1024)}, u32[]{:S(2)}) copy-start(s32[4096]{0:T(1024)} %param.14) | copy-start | bytes 49156
  3.2 13.1 %all-to-all-start = ((bf16[4,1024,64]{1,2,0:T(8,128)(2,1)}), bf16[4,1024,64]{1,2,0:T(8,128)(2,1)S(1)}, u32[]{:S(2)}, u32[]{:S(2)}) async-start(bf16[4,1024,64]{1,2,0:T(8,128)(2,1)} %fusion.4), calls=%async_computation | async-start | bytes 1048576 | tf_op jit(solution)/shard_map/all_to_all | solution.py:292
  48.8 14.7 %copy-start.1 = (f32[1,1024,128]{2,1,0:T(8,128)S(1)}, f32[1,1024,128]{2,1,0:T(8,128)}, u32[]{:S(2)}) copy-start(f32[1,1024,128]{2,1,0:T(8,128)} %param.12) | copy-start | bytes 1572868
  48.8 14.7 %copy-start.3 = (f32[4,64,128]{2,1,0:T(8,128)S(1)}, f32[4,64,128]{2,1,0:T(8,128)}, u32[]{:S(2)}) copy-start(f32[4,64,128]{2,1,0:T(8,128)} %constant.69.clone) | copy-start | bytes 393220
  48.8 14.7 %copy-start.5 = (f32[128]{0:T(128)S(1)}, f32[128]{0:T(128)}, u32[]{:S(2)}) copy-start(f32[128]{0:T(128)} %constant.68.clone) | copy-start | bytes 1540
  51.3 12.3 %all-to-all-start.1 = ((bf16[4,1024,64]{1,2,0:T(8,128)(2,1)}), bf16[4,1024,64]{1,2,0:T(8,128)(2,1)S(1)}, u32[]{:S(2)}, u32[]{:S(2)}) async-start(bf16[4,1024,64]{1,2,0:T(8,128)(2,1)} %copy.15), calls=%async_computation.1 | async-start | bytes 1048576 | tf_op jit(solution)/shard_map/all_to_all | solution.py:296
  54.8 37.7 %copy-start.2 = (bf16[8,131072]{1,0:T(8,128)(2,1)S(1)}, bf16[8,131072]{1,0:T(8,128)(2,1)}, u32[]{:S(2)}) copy-start(bf16[8,131072]{1,0:T(8,128)(2,1)} %param.15) | copy-start | bytes 6291460

commit v3 on v2

--- a/solution.py
+++ b/solution.py
@@ -53,9 +53,13 @@
     xw, yw, rows_ref, spread_ref, pot_ref, sy_ref, syt_ref, sx_ref, sxt_ref, out_ref, cols_ref, grid_ref, line_ref
 ):
     planes = pot_ref.shape[0]
-    cols = spread_ref.shape[0]
+    cols = cols_ref.shape[0]
     grid_ref[...] = jnp.zeros_like(grid_ref)
-    cols_ref[:, :planes] = spread_ref[...].astype(F32)
+    fold = 128 // planes
+    groups, packed = spread_ref.shape[:2]
+    spots = [(g, f, (g * fold + f) * packed) for g in range(groups) for f in range(fold)]
+    for g, f, base in spots:
+        cols_ref[base : base + packed, :planes] = spread_ref[g, :, f * planes : (f + 1) * planes].astype(F32)
 
     @loop(cols // 32)
     def _(step, carry):
@@ -102,19 +106,21 @@
             cols_ref[pl.ds(base + i, 1), :] = grid_ref[pl.ds(rows_ref[base + i], 1), :]
         return carry
 
-    out_ref[...] = cols_ref[:, :planes].astype(BF16)
+    for g in range(groups):
+        parts = [cols_ref[base : base + packed, :planes] for at, f, base in spots if at == g]
+        out_ref[g] = jnp.concatenate(parts, axis=1).astype(BF16)
 
 
 def apply_planes(rows, spread, potential, xw, yw):
     planes, size_x, size_y = potential.shape
-    cols = spread.shape[0]
+    cols = rows.shape[0]
     table_x = hartley(size_x)[:, (np.arange(xw) - xw // 2) % size_x]
     table_y = hartley(size_y)[:, (np.arange(yw) - yw // 2) % size_y]
     vmem = pl.BlockSpec(memory_space=pltpu.VMEM)
     cast = lambda a: jnp.asarray(a, BF16)
     return pl.pallas_call(
         functools.partial(plane_kernel, xw, yw),
-        out_shape=jax.ShapeDtypeStruct((cols, planes), BF16),
+        out_shape=jax.ShapeDtypeStruct(spread.shape, BF16),
         in_specs=[pl.BlockSpec(memory_space=pltpu.SMEM)] + [vmem] * 6,
         out_specs=vmem,
         scratch_shapes=[
@@ -126,14 +132,111 @@
     )(rows, spread, potential, cast(table_y.T), cast(table_y), cast(table_x), cast(table_x.T))
 
 
+def peer_hops(groups):
+    return sorted(range(1, groups), key=lambda hop: -min(hop, groups - hop))
+
+
+def spread_kernel(groups, coeffs_ref, table_ref, out_ref, stage_ref, own_sem, send_sem, recv_sem):
+    me = lax.axis_index("ga")
+    packed = out_ref.shape[1]
+    fold = coeffs_ref.shape[0] // packed
+
+    def transform(to):
+        table = table_ref[to]
+        parts = [
+            jnp.dot(coeffs_ref[f * packed : (f + 1) * packed, :].astype(BF16), table, preferred_element_type=F32)
+            for f in range(fold)
+        ]
+        return jnp.concatenate(parts, axis=1).astype(BF16)
+
+    barrier = pltpu.get_barrier_semaphore()
+    for hop in peer_hops(groups):
+        pl.semaphore_signal(
+            barrier,
+            inc=1,
+            device_id={"ga": (me + hop) % groups},
+            device_id_type=pl.DeviceIdType.MESH,
+        )
+    copies = []
+    for place, hop in enumerate(peer_hops(groups)):
+        to = (me + hop) % groups
+        stage_ref[hop] = transform(to)
+        if place == 0:
+            pl.semaphore_wait(barrier, groups - 1)
+        copy = pltpu.make_async_remote_copy(
+            src_ref=stage_ref.at[hop],
+            dst_ref=out_ref.at[me],
+            send_sem=send_sem.at[hop],
+            recv_sem=recv_sem.at[hop],
+            device_id={"ga": to},
+            device_id_type=pl.DeviceIdType.MESH,
+        )
+        copy.start()
+        copies.append(copy)
+    stage_ref[0] = transform(me)
+    own = pltpu.make_async_copy(stage_ref.at[0], out_ref.at[me], own_sem)
+    own.start()
+    own.wait()
+    for hop in peer_hops(groups):
+        at = out_ref.at[(me + groups - hop) % groups]
+        pltpu.make_async_copy(at, at, recv_sem.at[hop]).wait()
+    for copy in copies:
+        copy.wait_send()
+
+
+def spread_columns(coeffs, table_z, groups, planes):
+    col_count, slots = coeffs.shape
+    packed = col_count * planes // 128
+    table = table_z.reshape(groups, planes, slots).transpose(0, 2, 1)
+    vmem = pl.BlockSpec(memory_space=pltpu.VMEM)
+    return pl.pallas_call(
+        functools.partial(spread_kernel, groups),
+        out_shape=jax.ShapeDtypeStruct((groups, packed, 128), BF16),
+        in_specs=[vmem, vmem],
+        out_specs=pl.BlockSpec(memory_space=pl.ANY),
+        scratch_shapes=[
+            pltpu.VMEM((groups, packed, 128), BF16),
+            pltpu.SemaphoreType.DMA,
+            pltpu.SemaphoreType.DMA((groups,)),
+            pltpu.SemaphoreType.DMA((groups,)),
+        ],
+        compiler_params=pltpu.CompilerParams(
+            collective_id=1, has_side_effects=True, vmem_limit_bytes=32 * 2**20
+        ),
+    )(coeffs, jnp.asarray(table, BF16))
+
+
 def gather_kernel(
-    depth, width, pieces, own_ref, out_ref, own_sem, line_send, line_recv, cross_send, cross_recv
+    depth,
+    width,
+    pieces,
+    groups,
+    picked_ref,
+    coeffs_ref,
+    kinetic_ref,
+    table_ref,
+    h_ref,
+    out_ref,
+    back_ref,
+    own_ref,
+    own_sem,
+    back_own,
+    back_send,
+    back_recv,
+    line_send,
+    line_recv,
+    cross_send,
+    cross_recv,
 ):
     band = lax.axis_index("band")
     z = band // width
     x = band % width
     rows = own_ref.shape[0] // pieces
     ways = (1, -1)
+    me = lax.axis_index("ga")
+    packed = back_ref.shape[1]
+    fold = own_ref.shape[0] // packed
+    planes = 128 // fold
 
     def inside(at):
         return jnp.logical_and(at >= 0, at < depth)
@@ -199,7 +302,43 @@
             device_id_type=pl.DeviceIdType.MESH,
         )
     beside = jnp.where(z > 0, 1, 0) + jnp.where(z < depth - 1, 1, 0)
-    pl.semaphore_wait(barrier, beside + width - 1)
+    for hop in peer_hops(groups):
+        pl.semaphore_signal(
+            barrier,
+            inc=1,
+            device_id={"ga": (me + hop) % groups},
+            device_id_type=pl.DeviceIdType.MESH,
+        )
+    pl.semaphore_wait(barrier, beside + width + groups - 2)
+
+    sent = []
+    for hop in peer_hops(groups):
+        to = (me + hop) % groups
+        copy = pltpu.make_async_remote_copy(
+            src_ref=picked_ref.at[to],
+            dst_ref=back_ref.at[me],
+            send_sem=back_send.at[hop],
+            recv_sem=back_recv.at[hop],
+            device_id={"ga": to},
+            device_id_type=pl.DeviceIdType.MESH,
+        )
+        copy.start()
+        sent.append(copy)
+    mine = pltpu.make_async_copy(picked_ref.at[me], back_ref.at[me], back_own)
+    mine.start()
+    mine.wait()
+    for hop in peer_hops(groups):
+        at = back_ref.at[(me + groups - hop) % groups]
+        pltpu.make_async_copy(at, at, back_recv.at[hop]).wait()
+    for f in range(fold):
+        at = slice(f * packed, (f + 1) * packed)
+        lines = jnp.concatenate(
+            [back_ref[g, :, f * planes : (f + 1) * planes] for g in range(groups)], axis=1
+        )
+        total = jnp.dot(lines, table_ref[...], preferred_element_type=F32)
+        total = total + kinetic_ref[at, :] * coeffs_ref[at, :]
+        h_ref[at, :] = total
+        own_ref[at, :] = total.astype(BF16)
 
     own = pltpu.make_async_copy(own_ref, out_ref.at[band], own_sem)
     own.start()
@@ -223,6 +362,8 @@
                         for hop in range(1, width):
                             cross_copy(hop, way, d, piece).start()
 
+    for copy in sent:
+        copy.wait_send()
     own.wait()
     for d in range(depth):
         for piece in range(pieces):
@@ -242,21 +383,34 @@
                             cross_arrival(hop, way, d, piece).wait()
 
 
-def gather_panel(own, bands):
+def finish(picked, coeffs, kinetic, table_z, bands):
+    groups = picked.shape[0]
     width = bands // 4 if bands % 4 == 0 and bands > 4 else 1
     depth = bands // width
     pieces = 2
     line = pltpu.SemaphoreType.DMA((2, depth, pieces))
     cross = pltpu.SemaphoreType.DMA((max(width - 1, 1), 2, depth, pieces))
+    peers = pltpu.SemaphoreType.DMA((groups,))
+    one = pltpu.SemaphoreType.DMA
     anywhere = pl.BlockSpec(memory_space=pl.ANY)
+    vmem = pl.BlockSpec(memory_space=pltpu.VMEM)
     return pl.pallas_call(
-        functools.partial(gather_kernel, depth, width, pieces),
-        out_shape=jax.ShapeDtypeStruct((bands,) + own.shape, own.dtype),
-        in_specs=[anywhere],
-        out_specs=anywhere,
-        scratch_shapes=[pltpu.SemaphoreType.DMA, line, line, cross, cross],
-        compiler_params=pltpu.CompilerParams(collective_id=0, has_side_effects=True),
-    )(own)
+        functools.partial(gather_kernel, depth, width, pieces, groups),
+        out_shape=(
+            jax.ShapeDtypeStruct(coeffs.shape, F32),
+            jax.ShapeDtypeStruct((bands,) + coeffs.shape, BF16),
+        ),
+        in_specs=[anywhere, vmem, vmem, vmem],
+        out_specs=(vmem, anywhere),
+        scratch_shapes=[
+            pltpu.VMEM(picked.shape, BF16),
+            pltpu.VMEM(coeffs.shape, BF16),
+        ]
+        + [one, one, peers, peers, line, line, cross, cross],
+        compiler_params=pltpu.CompilerParams(
+            collective_id=0, has_side_effects=True, vmem_limit_bytes=32 * 2**20
+        ),
+    )(picked, coeffs, kinetic, jnp.asarray(table_z, BF16))
 
 
 def body(coeffs, potential, stick_cells, block, rotation):
@@ -285,19 +439,9 @@
     line_part = jnp.asarray(0.5 * (2.0 * math.pi / size_z) ** 2 * freq_z * freq_z, F32)
     kinetic = plane_part[:, None] + line_part[None, :]
 
-    table_f = jnp.asarray(table_z.reshape(groups, planes, slots), F32)
-    table_b = jnp.asarray(table_z.reshape(groups, planes, slots), F32)
-    high = lax.Precision.HIGH
-    sent = jnp.einsum("sk,gzk->gsz", coeffs[0], table_f, precision=high).astype(BF16)
-    spread = lax.all_to_all(sent, "ga", split_axis=0, concat_axis=0, tiled=True)
-    spread = spread.reshape(cols, planes)
+    spread = spread_columns(coeffs[0], table_z, groups, planes)
     picked = apply_planes(rows, spread, potential, xw, yw)
-    picked = picked.reshape(groups, col_count, planes)
-    returned = lax.all_to_all(picked, "ga", split_axis=0, concat_axis=0, tiled=True)
-    results = (
-        jnp.einsum("gsz,gzk->sk", returned.astype(F32), table_b, precision=high) + (kinetic + LEVEL) * coeffs[0]
-    )
-    panel = gather_panel(results.astype(BF16), lax.axis_size("band"))
+    results, panel = finish(picked, coeffs[0], kinetic + LEVEL, table_z, lax.axis_size("band"))
     summed = jnp.dot(
         rotation,
         panel.reshape(panel.shape[0], col_count * slots),

time: 97.1 us -> 86.7 us (0.89)
  Pallas kernels: 58.7 us -> 76.2 us
  waiting for transfers between devices: 17 us -> 0 us
  starting transfers between devices: 7.71 us -> 0 us
  matrix products: 8.31 us -> 2.73 us
  other arithmetic: 0.64 us -> 2.2 us
    pallas_call x1 -> x2, Pallas kernels: 27.4 us -> 44.9 us  [the longest x1 35.3 us: finish(): pl.pallas_call(functools.partial(gather_kernel, depth, width, pieces, gro...]
    all_to_all x2 -> x0, waiting for transfers between devices: 17 us -> none  [the longest x1 8.77 us: body(): lax.all_to_all(picked, 'ga', split_axis=0, concat_axis=0, tiled=True)]
    all_to_all x2 -> x0, starting transfers between devices: 7.71 us -> none  [the longest x1 4.24 us: body(): spread = lax.all_to_all(sent, 'ga', split_axis=0, concat_axis=0, tiled=True)]
    unnamed x12 -> x17, local copies, waits for them, and re-layouts: 0.03 us -> 4.58 us
    dot_general x2 -> x0, matrix products: 3.99 us -> none  [the longest x1 2.5 us: body(): jnp.einsum('sk,gzk->gsz', coeffs[0], table_f, precision=high).astype(BF16)]
    reshape x1 -> x0, local copies, waits for them, and re-layouts: 2.41 us -> none  [body(): picked = picked.reshape(groups, col_count, planes)]
    dot_general x1, matrix products: 4.32 us -> 2.73 us  [body(): jnp.dot(rotation, panel.reshape(panel.shape[0], col_count * slots), prefe...]
    all_to_all x1 -> x0, local copies, waits for them, and re-layouts: 1.31 us -> none  [body(): spread = lax.all_to_all(sent, 'ga', split_axis=0, concat_axis=0, tiled=True)]
  transfers between devices with their start and end apart: 2 -> 0, of which waited for: 2 -> 0; matrix products, arithmetic and copies ran while one was open for 1% -> 0% of each run, Pallas kernels for 0% -> 0%
where the time goes in v3:
time: 86.7 us; the launch traced here: 86.4 us
  Pallas kernels  76.2 us (88%)
  local copies, waits for them, and re-layouts  4.58 us (5%)
  matrix products  2.73 us (3%)
  other arithmetic  2.2 us (3%)
    pallas_call x1, Pallas kernels, finish(): pl.pallas_call(functools.partial(gather_kernel, depth, width, pieces, gro...  35.3 us
    pallas_call x1, Pallas kernels, apply_planes(): pl.pallas_call(functools.partial(plane_kernel, xw, yw), out_shape=jax.Sha...  31.2 us
    pallas_call x1, Pallas kernels, spread_columns(): pl.pallas_call(functools.partial(spread_kernel, groups), out_shape=jax.Sh...  9.63 us
    unnamed x17, local copies, waits for them, and re-layouts  4.58 us
    dot_general x1, matrix products, body(): jnp.dot(rotation, panel.reshape(panel.shape[0], col_count * slots), prefe...  2.73 us

profile of v3, /device:TPU:0, one launch (start us, length us, event | category | flops | bytes accessed | tf_op | source)
XLA Modules:
  0.0 86.4 jit_solution(9420522527969038313)
XLA Ops:
  0.6 0.0 copy-start
  0.7 1.3 %add_select_fusion.2 = (s32[4096]{0:T(1024)S(1)}, s32[4096]{0:T(1024)}, s32[4096]{0:T(1024)S(1)}) fusion(s32[4096]{0:T(1024)} %param.14), kind=kLoop, calls=%fused_computation.8 | loop fusion | flops 126976 | bytes 65536 | tf_op jit(solution)/shard_map/jit(_where)/select_n | solution.py:45
  2.0 0.8 add_add_fusion.kinetic_ref
  2.9 0.0 copy-start.2
  2.9 1.0 %copy-done.2 = f32[1,1024,128]{2,1,0:T(8,128)S(1)} copy-done((f32[1,1024,128]{2,1,0:T(8,128)S(1)}, f32[1,1024,128]{2,1,0:T(8,128)}, u32[]{:S(2)}) %copy-start.2) | copy-done | bytes 524312
  3.9 0.0 copy-start.5
  3.9 0.9 %copy-done.5 = bf16[4,128,64]{2,1,0:T(8,128)(2,1)S(1)} copy-done((bf16[4,128,64]{2,1,0:T(8,128)(2,1)S(1)}, bf16[4,128,64]{2,1,0:T(8,128)(2,1)}, u32[]{:S(2)}) %copy-start.5) | copy-done | bytes 65560
  4.8 9.6 %shard_map.131.spread_ref = bf16[4,512,128]{2,1,0:T(8,128)(2,1)S(1)} custom-call(f32[1024,128]{1,0:T(8,128)S(1)} %bitcast.13, bf16[4,128,64]{2,1,0:T(8,128)(2,1)S(1)} %copy-done.5), custom_call_target="tpu_custom_call" | custom-call | tf_op jit(solution)/shard_map/pallas_call | solution.py:192
  14.5 0.0 copy-start.4
  14.5 0.8 copy-done.4
  15.2 0.0 copy-start.3
  15.2 0.0 copy-start.6
  15.3 0.0 copy-start.7
  15.3 31.2 %shard_map.132.picked_ref = bf16[4,512,128]{2,1,0:T(8,128)(2,1)} custom-call(s32[4096]{0:T(1024)} %get-tuple-element.7.rows_ref, bf16[4,512,128]{2,1,0:T(8,128)(2,1)} %copy-done.4, bf16[64,256,256]{2,1,0:T(8,128)(2,1)} %pot_ref.1, bf16[128,256]{1,0:T(8,128)(2,1)} %constant.72.clone.sy_ref, bf16[256,128]{1,0:T(8,128)(2,1)} %constant.73.clone.syt_ref, ...), custom_call_target="tpu_custom_call" | custom-call | tf_op jit(solution)/shard_map/pallas_call | solution.py:121
  46.5 0.0 copy-done.3
  46.5 0.0 copy-done.6
  46.5 0.0 copy-start.1
  46.5 1.0 %copy-done.1 = bf16[4,512,128]{2,1,0:T(8,128)(2,1)S(1)} copy-done((bf16[4,512,128]{2,1,0:T(8,128)(2,1)S(1)}, bf16[4,512,128]{2,1,0:T(8,128)(2,1)}, u32[]{:S(2)}) %copy-start.1) | copy-done | bytes 524312
  47.5 35.3 %shard_map.133 = (f32[1024,128]{1,0:T(8,128)S(1)}, bf16[8,1024,128]{2,1,0:T(8,128)(2,1)S(1)}) custom-call(bf16[4,512,128]{2,1,0:T(8,128)(2,1)S(1)} %copy-done.1, f32[1024,128]{1,0:T(8,128)S(1)} %bitcast.14, f32[1024,128]{1,0:T(8,128)S(1)} %add_add_fusion.kinetic_ref, bf16[256,128]{1,0:T(8,128)(2,1)S(1)} %copy-done.6), custom_call_target="tpu_custom_call" | custom-call | tf_op jit(solution)/shard_map/pallas_call | solution.py:397
  82.9 0.0 copy-done
  82.9 0.0 copy-done.7
  82.9 2.7 %fusion.1 = bf16[8,131072]{1,0:T(8,128)(2,1)} fusion(bf16[8,8]{1,0:T(8,128)(2,1)S(1)} %copy-done, bf16[8,131072]{1,0:T(8,128)(2,1)S(1)} %copy-done.7, bf16[1,8,1024,128]{3,2,1,0:T(8,128)(2,1)S(1)} %bitcast.15), kind=kOutput, calls=%fused_computation.2 | convolution fusion | flops 19922944 | bytes 6291584 | tf_op jit(solution)/shard_map/dot_general | solution.py:445
  85.6 0.8 copy.20
  (1 shorter events, 0.0 us)
Async XLA Ops:
  0.6 82.2 %copy-start = (bf16[8,8]{1,0:T(8,128)(2,1)S(1)}, bf16[8,8]{1,0:T(8,128)(2,1)}, u32[]{:S(2)}) copy-start(bf16[8,8]{1,0:T(8,128)(2,1)} %param.16) | copy-start | bytes 388
  2.9 1.0 %copy-start.2 = (f32[1,1024,128]{2,1,0:T(8,128)S(1)}, f32[1,1024,128]{2,1,0:T(8,128)}, u32[]{:S(2)}) copy-start(f32[1,1024,128]{2,1,0:T(8,128)} %param.12) | copy-start | bytes 1572868
  3.9 0.9 %copy-start.5 = (bf16[4,128,64]{2,1,0:T(8,128)(2,1)S(1)}, bf16[4,128,64]{2,1,0:T(8,128)(2,1)}, u32[]{:S(2)}) copy-start(bf16[4,128,64]{2,1,0:T(8,128)(2,1)} %constant.71.clone.table_ref) | copy-start | bytes 196612
  14.5 0.8 copy-start.4
  15.2 31.3 %copy-start.3 = (f32[1,1024,128]{2,1,0:T(8,128)S(1)}, f32[1,1024,128]{2,1,0:T(8,128)}, u32[]{:S(2)}) copy-start(f32[1,1024,128]{2,1,0:T(8,128)} %param.12) | copy-start | bytes 1572868
  15.2 31.3 %copy-start.6 = (bf16[256,128]{1,0:T(8,128)(2,1)S(1)}, bf16[256,128]{1,0:T(8,128)(2,1)}, u32[]{:S(2)}) copy-start(bf16[256,128]{1,0:T(8,128)(2,1)} %constant.76.clone.table_ref) | copy-start | bytes 196612
  15.3 67.6 %copy-start.7 = (bf16[8,131072]{1,0:T(8,128)(2,1)S(1)}, bf16[8,131072]{1,0:T(8,128)(2,1)}, u32[]{:S(2)}) copy-start(bf16[8,131072]{1,0:T(8,128)(2,1)} %param.15) | copy-start | bytes 6291460
  46.5 1.0 %copy-start.1 = (bf16[4,512,128]{2,1,0:T(8,128)(2,1)S(1)}, bf16[4,512,128]{2,1,0:T(8,128)(2,1)}, u32[]{:S(2)}) copy-start(bf16[4,512,128]{2,1,0:T(8,128)(2,1)} %shard_map.132.picked_ref) | copy-start | bytes 1572868

commit v4 on v3

--- a/solution.py
+++ b/solution.py
@@ -12,7 +12,8 @@
 BF16 = jnp.bfloat16
 F32 = jnp.float32
 LEVEL = -0.5
-BATCH = 8
+BATCH = 16
+CUTS = 2
 
 
 def hartley(count):
@@ -57,9 +58,16 @@
     grid_ref[...] = jnp.zeros_like(grid_ref)
     fold = 128 // planes
     groups, packed = spread_ref.shape[:2]
-    spots = [(g, f, (g * fold + f) * packed) for g in range(groups) for f in range(fold)]
-    for g, f, base in spots:
-        cols_ref[base : base + packed, :planes] = spread_ref[g, :, f * planes : (f + 1) * planes].astype(F32)
+    part = packed // CUTS
+    spots = [
+        (g, c, f, ((g * CUTS + c) * fold + f) * part)
+        for g in range(groups)
+        for c in range(CUTS)
+        for f in range(fold)
+    ]
+    for g, c, f, base in spots:
+        held = spread_ref[g, c * part : (c + 1) * part, f * planes : (f + 1) * planes]
+        cols_ref[base : base + part, :planes] = held.astype(F32)
 
     @loop(cols // 32)
     def _(step, carry):
@@ -79,8 +87,8 @@
         halves = range(yw // 128)
         def join(parts):
             return parts[0] if len(parts) == 1 else jnp.concatenate(parts, axis=1)
-        part = jnp.concatenate([join([line_ref[h, at, :].astype(BF16) for h in halves]) for at in ats], axis=0)
-        lines = jnp.dot(part, sy_ref[...], preferred_element_type=F32).astype(BF16)
+        rows_in = jnp.concatenate([join([line_ref[h, at, :].astype(BF16) for h in halves]) for at in ats], axis=0)
+        lines = jnp.dot(rows_in, sy_ref[...], preferred_element_type=F32).astype(BF16)
         low = []
         for i in range(BATCH):
             field = jnp.dot(sx_ref[...], lines[i * xw : (i + 1) * xw], preferred_element_type=F32)
@@ -107,8 +115,9 @@
         return carry
 
     for g in range(groups):
-        parts = [cols_ref[base : base + packed, :planes] for at, f, base in spots if at == g]
-        out_ref[g] = jnp.concatenate(parts, axis=1).astype(BF16)
+        for c in range(CUTS):
+            parts = [cols_ref[base : base + part, :planes] for *at, _, base in spots if at == [g, c]]
+            out_ref[g, c * part : (c + 1) * part, :] = jnp.concatenate(parts, axis=1).astype(BF16)
 
 
 def apply_planes(rows, spread, potential, xw, yw):
@@ -143,11 +152,13 @@
 
     def transform(to):
         table = table_ref[to]
-        parts = [
-            jnp.dot(coeffs_ref[f * packed : (f + 1) * packed, :].astype(BF16), table, preferred_element_type=F32)
-            for f in range(fold)
+        part = packed // CUTS
+        lines = [
+            jnp.dot(coeffs_ref[i * part : (i + 1) * part, :].astype(BF16), table, preferred_element_type=F32)
+            for i in range(CUTS * fold)
         ]
-        return jnp.concatenate(parts, axis=1).astype(BF16)
+        lines = [jnp.concatenate(lines[c * fold : (c + 1) * fold], axis=1) for c in range(CUTS)]
+        return jnp.concatenate(lines, axis=0).astype(BF16)
 
     barrier = pltpu.get_barrier_semaphore()
     for hop in peer_hops(groups):
@@ -282,6 +293,24 @@
             out_ref.at[slot, cut, :], out_ref.at[slot, cut, :], cross_recv.at[hop - 1, way, d, piece]
         )
 
+    def pass_on(d, piece):
+        for way in range(2):
+
+            @pl.when(inside(z - ways[way] * d))
+            def _(way=way):
+                if d > 0:
+                    line_arrival(way, d, piece).wait()
+
+                if d < depth - 1:
+
+                    @pl.when(inside(z + ways[way]))
+                    def _():
+                        line_copy(way, d, piece).start()
+
+                if d > 0 or way == 0:
+                    for hop in range(1, width):
+                        cross_copy(hop, way, d, piece).start()
+
     barrier = pltpu.get_barrier_semaphore()
     for way in ways:
 
@@ -311,56 +340,47 @@
         )
     pl.semaphore_wait(barrier, beside + width + groups - 2)
 
+    part = packed // CUTS
     sent = []
-    for hop in peer_hops(groups):
-        to = (me + hop) % groups
-        copy = pltpu.make_async_remote_copy(
-            src_ref=picked_ref.at[to],
-            dst_ref=back_ref.at[me],
-            send_sem=back_send.at[hop],
-            recv_sem=back_recv.at[hop],
-            device_id={"ga": to},
-            device_id_type=pl.DeviceIdType.MESH,
-        )
-        copy.start()
-        sent.append(copy)
+    for c in range(CUTS):
+        cut = pl.ds(c * part, part)
+        for hop in peer_hops(groups):
+            to = (me + hop) % groups
+            copy = pltpu.make_async_remote_copy(
+                src_ref=picked_ref.at[to, cut, :],
+                dst_ref=back_ref.at[me, cut, :],
+                send_sem=back_send.at[hop, c],
+                recv_sem=back_recv.at[hop, c],
+                device_id={"ga": to},
+                device_id_type=pl.DeviceIdType.MESH,
+            )
+            copy.start()
+            sent.append(copy)
     mine = pltpu.make_async_copy(picked_ref.at[me], back_ref.at[me], back_own)
     mine.start()
     mine.wait()
-    for hop in peer_hops(groups):
-        at = back_ref.at[(me + groups - hop) % groups]
-        pltpu.make_async_copy(at, at, back_recv.at[hop]).wait()
-    for f in range(fold):
-        at = slice(f * packed, (f + 1) * packed)
-        lines = jnp.concatenate(
-            [back_ref[g, :, f * planes : (f + 1) * planes] for g in range(groups)], axis=1
-        )
-        total = jnp.dot(lines, table_ref[...], preferred_element_type=F32)
-        total = total + kinetic_ref[at, :] * coeffs_ref[at, :]
-        h_ref[at, :] = total
-        own_ref[at, :] = total.astype(BF16)
-
+    for c in range(CUTS):
+        for hop in peer_hops(groups):
+            at = back_ref.at[(me + groups - hop) % groups, pl.ds(c * part, part), :]
+            pltpu.make_async_copy(at, at, back_recv.at[hop, c]).wait()
+        for f in range(fold):
+            at = slice((c * fold + f) * part, (c * fold + f + 1) * part)
+            held = slice(c * part, (c + 1) * part)
+            lines = jnp.concatenate(
+                [back_ref[g, held, f * planes : (f + 1) * planes] for g in range(groups)], axis=1
+            )
+            total = jnp.dot(lines, table_ref[...], preferred_element_type=F32)
+            total = total + kinetic_ref[at, :] * coeffs_ref[at, :]
+            h_ref[at, :] = total
+            own_ref[at, :] = total.astype(BF16)
+        for piece in range(c * pieces // CUTS, (c + 1) * pieces // CUTS):
+            pass_on(0, piece)
     own = pltpu.make_async_copy(own_ref, out_ref.at[band], own_sem)
     own.start()
 
-    for d in range(depth):
+    for d in range(1, depth):
         for piece in range(pieces):
-            for way in range(2):
-
-                @pl.when(inside(z - ways[way] * d))
-                def _(way=way):
-                    if d > 0:
-                        line_arrival(way, d, piece).wait()
-
-                    if d < depth - 1:
-
-                        @pl.when(inside(z + ways[way]))
-                        def _():
-                            line_copy(way, d, piece).start()
-
-                    if d > 0 or way == 0:
-                        for hop in range(1, width):
-                            cross_copy(hop, way, d, piece).start()
+            pass_on(d, piece)
 
     for copy in sent:
         copy.wait_send()
@@ -387,10 +407,10 @@
     groups = picked.shape[0]
     width = bands // 4 if bands % 4 == 0 and bands > 4 else 1
     depth = bands // width
-    pieces = 2
+    pieces = 2 * CUTS
     line = pltpu.SemaphoreType.DMA((2, depth, pieces))
     cross = pltpu.SemaphoreType.DMA((max(width - 1, 1), 2, depth, pieces))
-    peers = pltpu.SemaphoreType.DMA((groups,))
+    peers = pltpu.SemaphoreType.DMA((groups, CUTS))
     one = pltpu.SemaphoreType.DMA
     anywhere = pl.BlockSpec(memory_space=pl.ANY)
     vmem = pl.BlockSpec(memory_space=pltpu.VMEM)

time: 86.7 us -> 84.3 us (0.972)
  Pallas kernels: 76.2 us -> 73.8 us
    pallas_call x1, Pallas kernels: 35.3 us -> 33.2 us  [finish(): pl.pallas_call(functools.partial(gather_kernel, depth, width, pieces, gro...]
where the time goes in v4:
time: 84.3 us; the launch traced here: 84 us
  Pallas kernels  73.8 us (88%)
  local copies, waits for them, and re-layouts  4.58 us (5%)
  matrix products  2.73 us (3%)
  other arithmetic  2.2 us (3%)
    pallas_call x1, Pallas kernels, finish(): pl.pallas_call(functools.partial(gather_kernel, depth, width, pieces, gro...  33.2 us
    pallas_call x1, Pallas kernels, apply_planes(): pl.pallas_call(functools.partial(plane_kernel, xw, yw), out_shape=jax.Sha...  30.9 us
    pallas_call x1, Pallas kernels, spread_columns(): pl.pallas_call(functools.partial(spread_kernel, groups), out_shape=jax.Sh...  9.63 us
    unnamed x17, local copies, waits for them, and re-layouts  4.58 us
    dot_general x1, matrix products, body(): jnp.dot(rotation, panel.reshape(panel.shape[0], col_count * slots), prefe...  2.73 us

profile of v4, /device:TPU:0, one launch (start us, length us, event | category | flops | bytes accessed | tf_op | source)
XLA Modules:
  0.0 84.0 jit_solution(742473264521409636)
XLA Ops:
  0.6 0.0 copy-start
  0.7 1.3 %add_select_fusion.2 = (s32[4096]{0:T(1024)S(1)}, s32[4096]{0:T(1024)}, s32[4096]{0:T(1024)S(1)}) fusion(s32[4096]{0:T(1024)} %param.14), kind=kLoop, calls=%fused_computation.8 | loop fusion | flops 126976 | bytes 65536 | tf_op jit(solution)/shard_map/jit(_where)/select_n | solution.py:46
  2.0 0.8 %add_add_fusion.kinetic_ref = f32[1024,128]{1,0:T(8,128)S(1)} fusion(f32[128]{0:T(128)} %constant.70.clone, f32[1024]{0:T(1024)S(1)} %fusion.7), kind=kLoop, calls=%fused_computation.5 | loop fusion | flops 262144 | bytes 528896 | tf_op jit(solution)/shard_map/add | solution.py:464
  2.9 0.0 copy-start.2
  2.9 1.0 %copy-done.2 = f32[1,1024,128]{2,1,0:T(8,128)S(1)} copy-done((f32[1,1024,128]{2,1,0:T(8,128)S(1)}, f32[1,1024,128]{2,1,0:T(8,128)}, u32[]{:S(2)}) %copy-start.2) | copy-done | bytes 524312
  3.9 0.0 copy-start.5
  3.9 0.9 %copy-done.5 = bf16[4,128,64]{2,1,0:T(8,128)(2,1)S(1)} copy-done((bf16[4,128,64]{2,1,0:T(8,128)(2,1)S(1)}, bf16[4,128,64]{2,1,0:T(8,128)(2,1)}, u32[]{:S(2)}) %copy-start.5) | copy-done | bytes 65560
  4.8 9.6 %shard_map.131.spread_ref = bf16[4,512,128]{2,1,0:T(8,128)(2,1)S(1)} custom-call(f32[1024,128]{1,0:T(8,128)S(1)} %bitcast.13, bf16[4,128,64]{2,1,0:T(8,128)(2,1)S(1)} %copy-done.5), custom_call_target="tpu_custom_call" | custom-call | tf_op jit(solution)/shard_map/pallas_call | solution.py:203
  14.5 0.0 copy-start.4
  14.5 0.8 copy-done.4
  15.2 0.0 copy-start.3
  15.2 0.0 copy-start.6
  15.3 0.0 copy-start.7
  15.3 30.9 %shard_map.132.picked_ref = bf16[4,512,128]{2,1,0:T(8,128)(2,1)} custom-call(s32[4096]{0:T(1024)} %get-tuple-element.7.rows_ref, bf16[4,512,128]{2,1,0:T(8,128)(2,1)} %copy-done.4, bf16[64,256,256]{2,1,0:T(8,128)(2,1)} %pot_ref.1, bf16[128,256]{1,0:T(8,128)(2,1)} %constant.72.clone.sy_ref, bf16[256,128]{1,0:T(8,128)(2,1)} %constant.73.clone.syt_ref, ...), custom_call_target="tpu_custom_call" | custom-call | tf_op jit(solution)/shard_map/pallas_call | solution.py:130
  46.1 0.0 copy-done.3
  46.1 0.0 copy-done.6
  46.1 0.0 copy-start.1
  46.2 1.0 %copy-done.1 = bf16[4,512,128]{2,1,0:T(8,128)(2,1)S(1)} copy-done((bf16[4,512,128]{2,1,0:T(8,128)(2,1)S(1)}, bf16[4,512,128]{2,1,0:T(8,128)(2,1)}, u32[]{:S(2)}) %copy-start.1) | copy-done | bytes 524312
  47.2 33.2 %shard_map.133 = (f32[1024,128]{1,0:T(8,128)S(1)}, bf16[8,1024,128]{2,1,0:T(8,128)(2,1)S(1)}) custom-call(bf16[4,512,128]{2,1,0:T(8,128)(2,1)S(1)} %copy-done.1, f32[1024,128]{1,0:T(8,128)S(1)} %bitcast.14, f32[1024,128]{1,0:T(8,128)S(1)} %add_add_fusion.kinetic_ref, bf16[256,128]{1,0:T(8,128)(2,1)S(1)} %copy-done.6), custom_call_target="tpu_custom_call" | custom-call | tf_op jit(solution)/shard_map/pallas_call | solution.py:417
  80.4 0.0 copy-done
  80.5 0.0 copy-done.7
  80.5 2.7 %fusion.1 = bf16[8,131072]{1,0:T(8,128)(2,1)} fusion(bf16[8,8]{1,0:T(8,128)(2,1)S(1)} %copy-done, bf16[8,131072]{1,0:T(8,128)(2,1)S(1)} %copy-done.7, bf16[1,8,1024,128]{3,2,1,0:T(8,128)(2,1)S(1)} %bitcast.15), kind=kOutput, calls=%fused_computation.2 | convolution fusion | flops 19922944 | bytes 6291584 | tf_op jit(solution)/shard_map/dot_general | solution.py:465
  83.2 0.8 copy.20
  (1 shorter events, 0.0 us)
Async XLA Ops:
  0.6 79.8 %copy-start = (bf16[8,8]{1,0:T(8,128)(2,1)S(1)}, bf16[8,8]{1,0:T(8,128)(2,1)}, u32[]{:S(2)}) copy-start(bf16[8,8]{1,0:T(8,128)(2,1)} %param.16) | copy-start | bytes 388
  2.9 1.0 %copy-start.2 = (f32[1,1024,128]{2,1,0:T(8,128)S(1)}, f32[1,1024,128]{2,1,0:T(8,128)}, u32[]{:S(2)}) copy-start(f32[1,1024,128]{2,1,0:T(8,128)} %param.12) | copy-start | bytes 1572868
  3.9 0.9 %copy-start.5 = (bf16[4,128,64]{2,1,0:T(8,128)(2,1)S(1)}, bf16[4,128,64]{2,1,0:T(8,128)(2,1)}, u32[]{:S(2)}) copy-start(bf16[4,128,64]{2,1,0:T(8,128)(2,1)} %constant.71.clone.table_ref) | copy-start | bytes 196612
  14.5 0.8 copy-start.4
  15.2 30.9 %copy-start.3 = (f32[1,1024,128]{2,1,0:T(8,128)S(1)}, f32[1,1024,128]{2,1,0:T(8,128)}, u32[]{:S(2)}) copy-start(f32[1,1024,128]{2,1,0:T(8,128)} %param.12) | copy-start | bytes 1572868
  15.2 30.9 %copy-start.6 = (bf16[256,128]{1,0:T(8,128)(2,1)S(1)}, bf16[256,128]{1,0:T(8,128)(2,1)}, u32[]{:S(2)}) copy-start(bf16[256,128]{1,0:T(8,128)(2,1)} %constant.76.clone.table_ref) | copy-start | bytes 196612
  15.3 65.2 %copy-start.7 = (bf16[8,131072]{1,0:T(8,128)(2,1)S(1)}, bf16[8,131072]{1,0:T(8,128)(2,1)}, u32[]{:S(2)}) copy-start(bf16[8,131072]{1,0:T(8,128)(2,1)} %param.15) | copy-start | bytes 6291460
  46.1 1.0 %copy-start.1 = (bf16[4,512,128]{2,1,0:T(8,128)(2,1)S(1)}, bf16[4,512,128]{2,1,0:T(8,128)(2,1)}, u32[]{:S(2)}) copy-start(bf16[4,512,128]{2,1,0:T(8,128)(2,1)} %shard_map.132.picked_ref) | copy-start | bytes 1572868

commit v5 on v4

--- a/solution.py
+++ b/solution.py
@@ -301,15 +301,15 @@
                 if d > 0:
                     line_arrival(way, d, piece).wait()
 
+                if d > 0 or way == 0:
+                    for hop in range(1, width):
+                        cross_copy(hop, way, d, piece).start()
+
                 if d < depth - 1:
 
                     @pl.when(inside(z + ways[way]))
                     def _():
                         line_copy(way, d, piece).start()
-
-                if d > 0 or way == 0:
-                    for hop in range(1, width):
-                        cross_copy(hop, way, d, piece).start()
 
     barrier = pltpu.get_barrier_semaphore()
     for way in ways:

time: 84.3 us -> 84.3 us (level)
  no operation moved by 1% of the time
where the time goes in v5:
time: 84.3 us; the launch traced here: 84 us
  Pallas kernels  73.8 us (88%)
  local copies, waits for them, and re-layouts  4.58 us (5%)
  matrix products  2.73 us (3%)
  other arithmetic  2.2 us (3%)
    pallas_call x1, Pallas kernels, finish(): pl.pallas_call(functools.partial(gather_kernel, depth, width, pieces, gro...  33.2 us
    pallas_call x1, Pallas kernels, apply_planes(): pl.pallas_call(functools.partial(plane_kernel, xw, yw), out_shape=jax.Sha...  30.9 us
    pallas_call x1, Pallas kernels, spread_columns(): pl.pallas_call(functools.partial(spread_kernel, groups), out_shape=jax.Sh...  9.63 us
    unnamed x17, local copies, waits for them, and re-layouts  4.58 us
    dot_general x1, matrix products, body(): jnp.dot(rotation, panel.reshape(panel.shape[0], col_count * slots), prefe...  2.73 us

profile of v5, /device:TPU:0, one launch (start us, length us, event | category | flops | bytes accessed | tf_op | source)
XLA Modules:
  0.0 84.0 jit_solution(16783143911828081596)
XLA Ops:
  0.6 0.0 copy-start
  0.7 1.3 %add_select_fusion.2 = (s32[4096]{0:T(1024)S(1)}, s32[4096]{0:T(1024)}, s32[4096]{0:T(1024)S(1)}) fusion(s32[4096]{0:T(1024)} %param.14), kind=kLoop, calls=%fused_computation.8 | loop fusion | flops 126976 | bytes 65536 | tf_op jit(solution)/shard_map/jit(_where)/select_n | solution.py:46
  2.0 0.8 %add_add_fusion.kinetic_ref = f32[1024,128]{1,0:T(8,128)S(1)} fusion(f32[128]{0:T(128)} %constant.70.clone, f32[1024]{0:T(1024)S(1)} %fusion.7), kind=kLoop, calls=%fused_computation.5 | loop fusion | flops 262144 | bytes 528896 | tf_op jit(solution)/shard_map/add | solution.py:464
  2.9 0.0 copy-start.2
  2.9 1.0 %copy-done.2 = f32[1,1024,128]{2,1,0:T(8,128)S(1)} copy-done((f32[1,1024,128]{2,1,0:T(8,128)S(1)}, f32[1,1024,128]{2,1,0:T(8,128)}, u32[]{:S(2)}) %copy-start.2) | copy-done | bytes 524312
  3.9 0.0 copy-start.5
  3.9 0.9 %copy-done.5 = bf16[4,128,64]{2,1,0:T(8,128)(2,1)S(1)} copy-done((bf16[4,128,64]{2,1,0:T(8,128)(2,1)S(1)}, bf16[4,128,64]{2,1,0:T(8,128)(2,1)}, u32[]{:S(2)}) %copy-start.5) | copy-done | bytes 65560
  4.8 9.6 %shard_map.131.spread_ref = bf16[4,512,128]{2,1,0:T(8,128)(2,1)S(1)} custom-call(f32[1024,128]{1,0:T(8,128)S(1)} %bitcast.13, bf16[4,128,64]{2,1,0:T(8,128)(2,1)S(1)} %copy-done.5), custom_call_target="tpu_custom_call" | custom-call | tf_op jit(solution)/shard_map/pallas_call | solution.py:203
  14.5 0.0 copy-start.4
  14.5 0.8 copy-done.4
  15.2 0.0 copy-start.3
  15.2 0.0 copy-start.6
  15.3 0.0 copy-start.7
  15.3 30.9 %shard_map.132.picked_ref = bf16[4,512,128]{2,1,0:T(8,128)(2,1)} custom-call(s32[4096]{0:T(1024)} %get-tuple-element.7.rows_ref, bf16[4,512,128]{2,1,0:T(8,128)(2,1)} %copy-done.4, bf16[64,256,256]{2,1,0:T(8,128)(2,1)} %pot_ref.1, bf16[128,256]{1,0:T(8,128)(2,1)} %constant.72.clone.sy_ref, bf16[256,128]{1,0:T(8,128)(2,1)} %constant.73.clone.syt_ref, ...), custom_call_target="tpu_custom_call" | custom-call | tf_op jit(solution)/shard_map/pallas_call | solution.py:130
  46.1 0.0 copy-done.3
  46.1 0.0 copy-done.6
  46.1 0.0 copy-start.1
  46.2 1.0 %copy-done.1 = bf16[4,512,128]{2,1,0:T(8,128)(2,1)S(1)} copy-done((bf16[4,512,128]{2,1,0:T(8,128)(2,1)S(1)}, bf16[4,512,128]{2,1,0:T(8,128)(2,1)}, u32[]{:S(2)}) %copy-start.1) | copy-done | bytes 524312
  47.2 33.2 %shard_map.133 = (f32[1024,128]{1,0:T(8,128)S(1)}, bf16[8,1024,128]{2,1,0:T(8,128)(2,1)S(1)}) custom-call(bf16[4,512,128]{2,1,0:T(8,128)(2,1)S(1)} %copy-done.1, f32[1024,128]{1,0:T(8,128)S(1)} %bitcast.14, f32[1024,128]{1,0:T(8,128)S(1)} %add_add_fusion.kinetic_ref, bf16[256,128]{1,0:T(8,128)(2,1)S(1)} %copy-done.6), custom_call_target="tpu_custom_call" | custom-call | tf_op jit(solution)/shard_map/pallas_call | solution.py:417
  80.4 0.0 copy-done
  80.5 0.0 copy-done.7
  80.5 2.7 %fusion.1 = bf16[8,131072]{1,0:T(8,128)(2,1)} fusion(bf16[8,8]{1,0:T(8,128)(2,1)S(1)} %copy-done, bf16[8,131072]{1,0:T(8,128)(2,1)S(1)} %copy-done.7, bf16[1,8,1024,128]{3,2,1,0:T(8,128)(2,1)S(1)} %bitcast.15), kind=kOutput, calls=%fused_computation.2 | convolution fusion | flops 19922944 | bytes 6291584 | tf_op jit(solution)/shard_map/dot_general | solution.py:465
  83.2 0.8 copy.20
  (1 shorter events, 0.0 us)
Async XLA Ops:
  0.6 79.8 %copy-start = (bf16[8,8]{1,0:T(8,128)(2,1)S(1)}, bf16[8,8]{1,0:T(8,128)(2,1)}, u32[]{:S(2)}) copy-start(bf16[8,8]{1,0:T(8,128)(2,1)} %param.16) | copy-start | bytes 388
  2.9 1.0 %copy-start.2 = (f32[1,1024,128]{2,1,0:T(8,128)S(1)}, f32[1,1024,128]{2,1,0:T(8,128)}, u32[]{:S(2)}) copy-start(f32[1,1024,128]{2,1,0:T(8,128)} %param.12) | copy-start | bytes 1572868
  3.9 0.9 %copy-start.5 = (bf16[4,128,64]{2,1,0:T(8,128)(2,1)S(1)}, bf16[4,128,64]{2,1,0:T(8,128)(2,1)}, u32[]{:S(2)}) copy-start(bf16[4,128,64]{2,1,0:T(8,128)(2,1)} %constant.71.clone.table_ref) | copy-start | bytes 196612
  14.5 0.8 copy-start.4
  15.2 30.9 %copy-start.3 = (f32[1,1024,128]{2,1,0:T(8,128)S(1)}, f32[1,1024,128]{2,1,0:T(8,128)}, u32[]{:S(2)}) copy-start(f32[1,1024,128]{2,1,0:T(8,128)} %param.12) | copy-start | bytes 1572868
  15.2 30.9 %copy-start.6 = (bf16[256,128]{1,0:T(8,128)(2,1)S(1)}, bf16[256,128]{1,0:T(8,128)(2,1)}, u32[]{:S(2)}) copy-start(bf16[256,128]{1,0:T(8,128)(2,1)} %constant.76.clone.table_ref) | copy-start | bytes 196612
  15.3 65.2 %copy-start.7 = (bf16[8,131072]{1,0:T(8,128)(2,1)S(1)}, bf16[8,131072]{1,0:T(8,128)(2,1)}, u32[]{:S(2)}) copy-start(bf16[8,131072]{1,0:T(8,128)(2,1)} %param.15) | copy-start | bytes 6291460
  46.1 1.0 %copy-start.1 = (bf16[4,512,128]{2,1,0:T(8,128)(2,1)S(1)}, bf16[4,512,128]{2,1,0:T(8,128)(2,1)}, u32[]{:S(2)}) copy-start(bf16[4,512,128]{2,1,0:T(8,128)(2,1)} %shard_map.132.picked_ref) | copy-start | bytes 1572868
